TPU v7x, 32 devices: a whole 2x2x4 slice. The times are simulated.
32 devices in a mesh: groups: 2 (over x), tx: 16 (over z, y, core).
Axes of the slice: x: 2, y: 2, z: 4, core: 2. Of those that a mesh axis runs over, the one named last changes fastest.
Arguments:
- voltage: float32 [256, 16, 1024], P(('groups', 'tx')), parts along dimension 0, may hold values from -3 to 3
- gating: float32 [256, 16, 1024], P(('groups', 'tx')), parts along dimension 0, may hold values from 0.05 to 0.95
- recovery: float32 [256, 16, 1024], P(('groups', 'tx')), parts along dimension 0, may hold values from -3 to 3
- tangents: float32 [8, 3, 256, 16, 1024], P(None, None, ('groups', 'tx')), parts along dimension 2, may hold values from -6 to 6
- parameters: float32 [16], P('groups'), parts along dimension 0, may hold values from 0.5 to 2
- region: int32 [256, 16, 1024], P(('groups', 'tx')), parts along dimension 0, may hold values from 0 to 7
- fiber_class: int32 [256, 16, 1024], P(('groups', 'tx')), parts along dimension 0, may hold values from 0 to 3
- electrode_site: int32 [8192], P(('groups', 'tx')), parts along dimension 0, may hold values from 0 to 8191
- electrode_owner: int32 [8192, 1], P(('groups', 'tx')), parts along dimension 0, may hold values from 0 to 15; in each aligned block of 256 rows (0 to 255, 256 to 511, ...) at most 16 rows name the same one
Outputs:
- tangents_out: float32 [8, 3, 256, 16, 1024], P(None, None, ('groups', 'tx')), parts along dimension 2
- jacobian: float32 [8192, 128], P(('groups', 'tx')), parts along dimension 0
There are 2 independent parts, one for each index of `groups`. A program takes and returns all parts, laid end to end along the dimension named above; each array names one. Nothing has to cross between parts.
Inputs may be any that keep to these rules, and one draw needn't show every extreme that they name: `electrode_owner`: among the electrodes of one tile at most 16 have the same owner, and in every draw some tile sends exactly 16 to one owner.
All inputs are finite; a program needn't handle non-finite values.
Results may differ from a plain program's by a relative error of at most 0.00002.
Values sent between devices are 32-bit elements; how exact they have to be, the bound alone decides.
No kernel may reach another device: no remote copies, remote signals or barrier semaphores. Data moves between devices by JAX's collectives and lax.ppermute only.
A program may use at most 192 MiB of HBM per device.

v0:
```python
import jax
import jax.numpy as jnp
from jax import lax
from jax.sharding import PartitionSpec as P

CAP = 16


TIME_STEP = 0.1
ION_SCALE = 2.0
GATE_RATE = 0.25
RECOVERY_RATE = 0.5
RECOVERY_DECAY = 0.8
COND_ALONG = 1.0
COND_ACROSS = 0.25
COND_DEPTH = 0.25
GATE_STEEP = 4.0


def padded_2(cells, sides, width):
    for axis, dim in sides:
        count = lax.axis_size(axis)
        ends = count - 1
        head = lax.slice_in_dim(cells, 0, width, axis=dim)
        tail = lax.slice_in_dim(cells, cells.shape[dim] - width, cells.shape[dim], axis=dim)
        cells = jnp.concatenate(
            [
                lax.ppermute(tail, axis, [(i, (i + 1) % count) for i in range(ends)]),
                cells,
                lax.ppermute(head, axis, [((i + 1) % count, i) for i in range(ends)]),
            ],
            axis=dim,
        )
    return cells


def conduct(fiber_class):
    along = jnp.where(fiber_class == 0, 1.0, jnp.where(fiber_class == 2, 0.0, 0.5)).astype(
        jnp.float32
    )
    oblique = jnp.where(fiber_class == 1, 0.5, jnp.where(fiber_class == 3, -0.5, 0.0)).astype(
        jnp.float32
    )
    spread_gap = COND_ALONG - COND_ACROSS
    return (
        COND_ACROSS + spread_gap * along,
        COND_ACROSS + spread_gap * (1.0 - along),
        spread_gap * oblique,
    )


def regional(region, parameters):
    labels = jnp.arange(parameters.shape[0], dtype=jnp.int32)
    member = (region[None] == labels[:, None, None, None]).astype(jnp.float32)
    return (member, jnp.sum(member * parameters[:, None, None, None], axis=0))


def spread(padded, coeffs):
    coef_xx, coef_yy, coef_xy = coeffs
    zeros_y = [(0, 0)] * (padded.ndim - 1) + [(1, 1)]
    y_padded = jnp.pad(padded, zeros_y)
    centre = padded[..., 1:-1, :, :]
    along_x = y_padded[..., 2:, :, 1:-1] - 2.0 * centre + y_padded[..., :-2, :, 1:-1]
    along_y = y_padded[..., 1:-1, :, 2:] - 2.0 * centre + y_padded[..., 1:-1, :, :-2]
    cross_xy = (
        y_padded[..., 2:, :, 2:]
        - y_padded[..., 2:, :, :-2]
        - y_padded[..., :-2, :, 2:]
        + y_padded[..., :-2, :, :-2]
    )
    z_above = jnp.concatenate([centre[..., 1:, :], centre[..., -1:, :]], axis=-2)
    z_below = jnp.concatenate([centre[..., :1, :], centre[..., :-1, :]], axis=-2)
    along_z = z_above - 2.0 * centre + z_below
    return coef_xx * along_x + coef_yy * along_y + 0.5 * coef_xy * cross_xy + COND_DEPTH * along_z


def advance(stacked, gating, recovery, tan_h, tan_c, coeffs, member, local_gain):
    diffusion = spread(stacked, coeffs)
    potential = stacked[0, 1:-1]
    tan_v = stacked[1:, 1:-1]
    current = potential - potential * potential * potential / 3.0
    current_slope = 1.0 - potential * potential
    gate_target = jax.nn.sigmoid(GATE_STEEP * potential)
    gate_slope = GATE_STEEP * gate_target * (1.0 - gate_target)
    ionic_gain = ION_SCALE * local_gain
    potential_new = potential + TIME_STEP * (
        diffusion[0] + ionic_gain * gating * current - recovery
    )
    gating_new = gating + GATE_RATE * (gate_target - gating)
    recovery_new = recovery + TIME_STEP * RECOVERY_RATE * (potential - RECOVERY_DECAY * recovery)
    tan_v_new = tan_v + TIME_STEP * (
        diffusion[1:]
        + ionic_gain * (gating * current_slope * tan_v + current * tan_h)
        + ION_SCALE * member * gating * current
        - tan_c
    )
    tan_h_new = tan_h + GATE_RATE * (gate_slope * tan_v - tan_h)
    tan_c_new = tan_c + TIME_STEP * RECOVERY_RATE * (tan_v - RECOVERY_DECAY * tan_c)
    return (potential_new, gating_new, recovery_new, tan_v_new, tan_h_new, tan_c_new)


def shards(
    voltage,
    gating,
    recovery,
    tangents,
    parameters,
    region,
    fiber_class,
    electrode_site,
    electrode_owner,
):
    row_width = voltage.shape[2]
    tile_count = lax.axis_size("tx")
    tan_v = tangents[:, 0]
    tan_h = tangents[:, 1]
    tan_c = tangents[:, 2]
    coeffs = conduct(fiber_class)
    member, local_gain = regional(region, parameters)
    for repeat in range(2):
        stacked = jnp.concatenate([voltage[None], tan_v], axis=0)
        stacked = padded_2(stacked, (("tx", 1),), 1)
        voltage, gating, recovery, tan_v, tan_h, tan_c = advance(
            stacked, gating, recovery, tan_h, tan_c, coeffs, member, local_gain
        )
    tangents_out = jnp.stack([tan_v, tan_h, tan_c], axis=1)
    owners = electrode_owner[:, 0]
    probe_rows = tan_v[:, electrode_site // row_width, :, electrode_site % row_width]
    probe_rows = probe_rows.reshape(probe_rows.shape[0], -1)
    row_size = probe_rows.shape[1]
    chosen = (owners[:, None] == jnp.arange(tile_count, dtype=jnp.int32)[None, :]).astype(jnp.int32)
    slot_rank = jnp.sum((jnp.cumsum(chosen, axis=0) - 1) * chosen, axis=1)
    target = owners * CAP + slot_rank
    outgoing = jnp.zeros((tile_count * CAP, row_size), jnp.float32).at[target].set(probe_rows)
    arrived = lax.all_to_all(
        outgoing.reshape(tile_count, CAP, row_size), "tx", split_axis=0, concat_axis=0, tiled=True
    )
    jacobian = arrived.reshape(tile_count * CAP, row_size)
    return (tangents_out, jacobian)


def solution(mesh):
    placed = (
        P(("groups", "tx"), None, None),
        P(("groups", "tx"), None, None),
        P(("groups", "tx"), None, None),
        P(None, None, ("groups", "tx"), None, None),
        P("groups"),
        P(("groups", "tx"), None, None),
        P(("groups", "tx"), None, None),
        P(("groups", "tx")),
        P(("groups", "tx"), None),
    )
    return jax.shard_map(
        shards,
        mesh=mesh,
        in_specs=placed,
        out_specs=(P(None, None, ("groups", "tx"), None, None), P(("groups", "tx"), None)),
        check_vma=False,
    )
```

profile of v0, /device:TPU:0, one launch (start us, length us, event | category | flops | bytes accessed | tf_op | source)
XLA Modules:
  0.0 174.4 jit_solution(6265154021442310276)
XLA Ops:
  0.6 2.6 %slice_bitcast_fusion = f32[8,8,16,1024]{3,2,1,0:T(8,128)S(1)} fusion(f32[8,3,8,16,1024]{4,3,2,1,0:T(8,128)} %param.12), kind=kLoop, calls=%fused_computation.112 | loop fusion | bytes 8388608 | tf_op jit(solution)/shard_map/squeeze | solution.py:115
  3.2 1.0 fusion.48
  4.2 1.4 collective-permute-start
  5.6 3.9 %collective-permute-start.1 = (f32[9,1,16,1024]{3,2,1,0:T(8,128)S(1)}, f32[9,1,16,1024]{3,2,1,0:T(8,128)}, u32[]{:S(2)}, u32[]{:S(2)}) collective-permute-start(f32[9,1,16,1024]{3,2,1,0:T(8,128)S(1)} %get-tuple-element.32), channel_id=1, source_target_pairs={{0,1},{1,2},{2,3},{3,4},{4,5},{5,6},{6,7},{7,8},{8,9},{9,10},{10,1... | collective-permute-start | bytes 1769480 | tf_op jit(solution)/shard_map/ppermute | solution.py:28
  9.5 1.4 fusion.62
  10.9 1.0 multiply_add_fusion.2
  12.8 1.3 select_reduce_fusion
  14.1 1.9 %multiply_add_fusion.1 = f32[8,16,1024]{2,1,0:T(8,128)} fusion(pred[8,16,1024]{2,1,0:T(8,128)(4,1)} %get-tuple-element.13, pred[8,16,1024]{2,1,0:T(8,128)(4,1)S(1)} %get-tuple-element.12), kind=kLoop, calls=%fused_computation.137 | loop fusion | flops 655360 | bytes 786432 | tf_op jit(solution)/shard_map/add | solution.py:47
  16.0 6.9 %fusion.6 = (f32[9,8,15,1024]{3,2,1,0:T(8,128)}, f32[9,8,15,1024]{3,2,1,0:T(8,128)}) fusion(f32[1,8,16,1024]{3,2,1,0:T(8,128)S(1)} %bitcast.108, f32[8,8,16,1024]{3,2,1,0:T(8,128)} %copy-done.2), kind=kLoop, calls=%fused_computation.33 | loop fusion | flops 2211840 | bytes 13565952 | tf_op jit(solution)/shard_map/concatenate | solution.py:121
  22.9 0.8 copy-done.13
  23.8 3.9 %select_maximum_fusion.3 = f32[9,10,16,1026]{3,2,1,0:T(8,128)S(1)} fusion(f32[9,1,16,1024]{3,2,1,0:T(8,128)} %copy-done.13, f32[9,1,16,1024]{3,2,1,0:T(8,128)} %collective-permute-done.1, f32[8,8,16,1024]{3,2,1,0:T(8,128)S(1)} %copy-done.3, f32[1,8,16,1024]{3,2,1,0:T(8,128)S(1)} %bitcast.109), kind=kLoop, calls=%fused_computation.22 | loop fusion | flops 14774400 | bytes 11808000 | tf_op jit(solution)/shard_map/concatenate | solution.py:26
  27.7 13.7 %fusion.9 = f32[9,8,16,1024]{3,2,1,0:T(8,128)} fusion(f32[9,10,16,1026]{3,2,1,0:T(8,128)S(1)} %select_maximum_fusion.3, f32[9,1,16,1024]{3,2,1,0:T(8,128)} %collective-permute-done.1, f32[8,8,16,1024]{3,2,1,0:T(8,128)} %copy-done.2, f32[1,8,16,1024]{3,2,1,0:T(8,128)S(1)} %bitcast.110, f32[9,1,16,1024]{3,2,1,0:T(8,128)} %copy-done.13, ...), kind=kLoop, calls=%fused_computation.41 | loop fusion | flops 28311552 | bytes 49938432 | tf_op jit(solution)/shard_map/add | solution.py:74
  41.4 3.2 %fusion.52 = (f32[8,16,1024]{2,1,0:T(8,128)}, f32[8,16,1024]{2,1,0:T(8,128)}, f32[8,16,1024]{2,1,0:T(8,128)S(1)}, f32[8,16,1024]{2,1,0:T(8,128)S(1)}, f32[8,16,1...) fusion(f32[8,16,1024]{2,1,0:T(8,128)} %param.10, f32[8,16,1024]{2,1,0:T(8,128)S(1)} %copy-done.4, ...), kind=kLoop, calls=%fused_computation.124 | loop fusion | flops 3407872 | bytes 6291456 | tf_op jit(solution)/shard_map/mul | solution.py:93
  44.6 1.0 fusion.54
  45.6 7.4 %add_bitcast_fusion.1 = (f32[8,1,8,16,1024]{4,3,2,1,0:T(8,128)}, f32[8,8,16,1024]{3,2,1,0:T(8,128)S(1)}) fusion(f32[8,16,1024]{2,1,0:T(8,128)S(1)} %get-tuple-element.37, f32[8,16,1024]{2,1,0:T(8,128)S(1)} %get-tuple-element.39, f32[8,3,8,16,1024]{4,3,2,1,0:T(8,128)} %param.12, f32[8,16,1024]{2,1,0:T(8,128)S(1)} %copy-done.15, ...), kind=kLoop, calls=%fused_computation.109 | loop fusion | flops 22020096 | bytes 28835840 | tf_op jit(solution)/shard_map/stack | solution.py:126
  53.2 5.1 %fusion.2 = (f32[9,8,15,1024]{3,2,1,0:T(8,128)}, f32[9,8,15,1024]{3,2,1,0:T(8,128)}) fusion(f32[1,8,16,1024]{3,2,1,0:T(8,128)S(1)} %bitcast.101, f32[8,8,16,1024]{3,2,1,0:T(8,128)S(1)} %get-tuple-element.10), kind=kLoop, calls=%fused_computation.29 | loop fusion | flops 2211840 | bytes 13565952 | tf_op jit(solution)/shard_map/concatenate | solution.py:121
  58.2 1.5 collective-permute-start.2
  59.8 4.9 %collective-permute-start.3 = (f32[9,1,16,1024]{3,2,1,0:T(8,128)S(1)}, f32[9,1,16,1024]{3,2,1,0:T(8,128)S(1)}, u32[]{:S(2)}, u32[]{:S(2)}) collective-permute-start(f32[9,1,16,1024]{3,2,1,0:T(8,128)S(1)} %get-tuple-element.26), channel_id=1, source_target_pairs={{0,1},{1,2},{2,3},{3,4},{4,5},{5,6},{6,7},{7,8},{8,9},{9,10},{10,1... | collective-permute-start | bytes 1769480 | tf_op jit(solution)/shard_map/ppermute | solution.py:28
  64.7 1.4 fusion.59
  66.2 3.5 %add_bitcast_fusion = f32[8,1,8,16,1024]{4,3,2,1,0:T(8,128)} fusion(f32[8,8,16,1024]{3,2,1,0:T(8,128)S(1)} %get-tuple-element.10, f32[8,3,8,16,1024]{4,3,2,1,0:T(8,128)S(1)} %bitcast.98), kind=kLoop, calls=%fused_computation.108 | loop fusion | flops 8388608 | bytes 16777216 | tf_op jit(solution)/shard_map/stack | solution.py:126
  69.7 0.8 copy-done.14
  70.6 4.5 %select_maximum_fusion = f32[9,10,16,1026]{3,2,1,0:T(8,128)} fusion(f32[9,1,16,1024]{3,2,1,0:T(8,128)S(1)} %collective-permute-done.2, f32[9,1,16,1024]{3,2,1,0:T(8,128)S(1)} %collective-permute-done.3, f32[8,8,16,1024]{3,2,1,0:T(8,128)S(1)} %get-tuple-element.10, f32[1,8,16,1024]{3,2,1,0:T(8,128)S(1)} %bitcast.103), kind=kLoop, calls=%fused_computation.19 | loop fusion | flops 14774400 | bytes 11808000 | tf_op jit(solution)/shard_map/concatenate | solution.py:26
  75.1 18.1 %fusion.73 = (f32[9,8,16,1024]{3,2,1,0:T(8,128)}, f32[9,8,16,1024]{3,2,1,0:T(8,128)}, f32[9,8,16,1024]{3,2,1,0:T(8,128)}, f32[9,8,16,1024]{3,2,1,0:T(8,128)}, f3...) fusion(f32[9,10,16,1026]{3,2,1,0:T(8,128)} %select_maximum_fusion), kind=kLoop, calls=%fused_computation.168 | loop fusion | bytes 56623104 | tf_op jit(solution)/shard_map/slice | solution.py:64
  93.2 7.8 %fusion.1 = (f32[9,8,16,1024]{3,2,1,0:T(8,128)}, f32[9,8,16,1024]{3,2,1,0:T(8,128)}) fusion(f32[1,8,16,1024]{3,2,1,0:T(8,128)S(1)} %bitcast.104, f32[8,8,16,1024]{3,2,1,0:T(8,128)} %copy-done, f32[9,1,16,1024]{3,2,1,0:T(8,128)} %copy-done.12), kind=kLoop, calls=%fused_computation.28 | loop fusion | flops 4718592 | bytes 14745600 | tf_op jit(solution)/shard_map/mul | solution.py:63
  101.1 1.5 copy-done.6
  102.6 1.3 copy-done.7
  104.1 19.5 %fusion.28 = f32[8,8,16,1024]{3,2,1,0:T(8,128)} fusion(f32[8,8,16,1024]{3,2,1,0:T(8,128)S(1)} %copy-done.1, f32[1,8,16,1024]{3,2,1,0:T(8,128)S(1)} %bitcast.105, f32[9,8,15,1024]{3,2,1,0:T(8,128)} %get-tuple-element.23, f32[9,8,1,1024]{3,2,1,0:T(1,128)} %get-tuple-element.25, f32[9,8,16,1024]{3,2,1,0:T(8,128)} %get-tuple-element.19, ...), kind=kLoop, calls=%fused_computation.77 | loop fusion | flops 42991616 | bytes 69795840 | tf_op jit(solution)/shard_map/add | solution.py:91
  123.6 18.4 %copy.292 = f32[8,8,16,1024]{2,0,3,1:T(8,128)} copy(f32[8,8,16,1024]{3,2,1,0:T(8,128)} %fusion.28) | data formatting | bytes 8388608 | tf_op jit(solution)/shard_map/add | solution.py:91
  142.0 2.4 %gather_fusion = f32[256,8,16]{2,1,0:T(8,128)S(1)} fusion(f32[8,8,16,1024]{2,0,3,1:T(8,128)} %copy.292, s32[256]{0:T(256)S(1)} %fusion.70), kind=kCustom, calls=%fused_computation | custom fusion | bytes 264192 | tf_op jit(solution)/shard_map/gather | solution.py:128
  144.9 1.8 %scatter_custom_fusion = f32[256,128]{1,0:T(8,128)} fusion(s32[256]{0:T(256)S(1)} %bitcast.116, f32[256,128]{1,0:T(8,128)S(1)} %copy.294, f32[]{:T(128)} %constant.29.clone.1), kind=kCustom, calls=%fused_computation.147 | custom fusion | bytes 131076 | tf_op jit(solution)/shard_map/scatter | solution.py:134
  146.6 14.9 %all-to-all-start = ((f32[16,16,128]{2,1,0:T(8,128)}), f32[16,16,128]{2,1,0:T(8,128)S(1)}, u32[]{:S(2)}, u32[]{:S(2)}) async-start(f32[16,16,128]{2,1,0:T(8,128)} %bitcast.18), calls=%async_computation | async-start | bytes 262144 | tf_op jit(solution)/shard_map/all_to_all | solution.py:135
  161.5 12.2 %pad_maximum_fusion.2 = f32[8,3,8,16,1024]{4,3,2,1,0:T(8,128)} fusion(f32[8,1,8,16,1024]{4,3,2,1,0:T(8,128)} %add_bitcast_fusion, f32[8,1,8,16,1024]{4,3,2,1,0:T(8,128)} %get-tuple-element.9, f32[8,1,8,16,1024]{4,3,2,1,0:T(8,128)} %bitcast.99), kind=kLoop, calls=%fused_computation.16 | loop fusion | flops 6291456 | bytes 25165824 | tf_op jit(solution)/shard_map/stack | solution.py:126
  (60 shorter events, 2.4 us)
Async XLA Ops:
  0.6 2.6 %copy-start.4 = (f32[8,16,1024]{2,1,0:T(8,128)S(1)}, f32[8,16,1024]{2,1,0:T(8,128)}, u32[]{:S(2)}) copy-start(f32[8,16,1024]{2,1,0:T(8,128)} %param.9) | copy-start | bytes 1572868
  3.2 7.7 %copy-start.2 = (f32[8,8,16,1024]{3,2,1,0:T(8,128)}, f32[8,8,16,1024]{3,2,1,0:T(8,128)S(1)}, u32[]{:S(2)}) copy-start(f32[8,8,16,1024]{3,2,1,0:T(8,128)S(1)} %slice_bitcast_fusion) | copy-start | bytes 12582916
  3.2 7.7 %copy-start.16 = (s32[8,16,1024]{2,1,0:T(8,128)S(1)}, s32[8,16,1024]{2,1,0:T(8,128)}, u32[]{:S(2)}) copy-start(s32[8,16,1024]{2,1,0:T(8,128)} %param.15) | copy-start | bytes 1572868
  4.2 7.7 %copy-start.18 = (s32[256]{0:T(256)S(1)}, s32[256]{0:T(256)}, u32[]{:S(2)}) copy-start(s32[256]{0:T(256)} %param.16) | copy-start | bytes 3076
  4.2 7.7 %copy-start.17 = (s32[256,1]{0,1:T(1,128)S(1)}, s32[256,1]{0,1:T(1,128)}, u32[]{:S(2)}) copy-start(s32[256,1]{0,1:T(1,128)} %param.17) | copy-start | bytes 3076
  4.2 8.6 %copy-start.9 = (s32[8,16,1024]{2,1,0:T(8,128)S(1)}, s32[8,16,1024]{2,1,0:T(8,128)}, u32[]{:S(2)}) copy-start(s32[8,16,1024]{2,1,0:T(8,128)} %param.14) | copy-start | bytes 1572868
  4.2 8.6 %copy-start.19 = (f32[8]{0:T(128)S(1)}, f32[8]{0:T(128)}, u32[]{:S(2)}) copy-start(f32[8]{0:T(128)} %param.13) | copy-start | bytes 100
  4.2 18.7 %collective-permute-start = (f32[9,1,16,1024]{3,2,1,0:T(8,128)}, f32[9,1,16,1024]{3,2,1,0:T(8,128)S(1)}, u32[]{:S(2)}, u32[]{:S(2)}) collective-permute-start(f32[9,1,16,1024]{3,2,1,0:T(8,128)} %get-tuple-element.33), channel_id=1, source_target_pairs={{1,0},{2,1},{3,2},{4,3},{5,4},{6,5},{7,6},{8,7},{9,8},{10,9},{11,1... | collective-permute-start | bytes 1769480 | tf_op jit(solution)/shard_map/ppermute | solution.py:30
  5.6 18.1 %collective-permute-start.1 = (f32[9,1,16,1024]{3,2,1,0:T(8,128)S(1)}, f32[9,1,16,1024]{3,2,1,0:T(8,128)}, u32[]{:S(2)}, u32[]{:S(2)}) collective-permute-start(f32[9,1,16,1024]{3,2,1,0:T(8,128)S(1)} %get-tuple-element.32), channel_id=1, source_target_pairs={{0,1},{1,2},{2,3},{3,4},{4,5},{5,6},{6,7},{7,8},{8,9},{9,10},{10,1... | collective-permute-start | bytes 1769480 | tf_op jit(solution)/shard_map/ppermute | solution.py:28
  16.0 7.7 %copy-start.3 = (f32[8,8,16,1024]{3,2,1,0:T(8,128)S(1)}, f32[8,8,16,1024]{3,2,1,0:T(8,128)}, u32[]{:S(2)}) copy-start(f32[8,8,16,1024]{3,2,1,0:T(8,128)} %copy-done.2) | copy-start | bytes 12582916
  22.9 0.8 copy-start.13
  41.4 4.2 %copy-start.5 = (f32[9,8,16,1024]{3,2,1,0:T(8,128)S(1)}, f32[9,8,16,1024]{3,2,1,0:T(8,128)}, u32[]{:S(2)}) copy-start(f32[9,8,16,1024]{3,2,1,0:T(8,128)} %fusion.9) | copy-start | bytes 14155780
  41.4 4.2 %copy-start.10 = (s32[8,16,1024]{2,1,0:T(8,128)S(1)}, s32[8,16,1024]{2,1,0:T(8,128)}, u32[]{:S(2)}) copy-start(s32[8,16,1024]{2,1,0:T(8,128)} %param.14) | copy-start | bytes 1572868
  41.4 4.2 %copy-start.15 = (f32[8,16,1024]{2,1,0:T(8,128)S(1)}, f32[8,16,1024]{2,1,0:T(8,128)}, u32[]{:S(2)}) copy-start(f32[8,16,1024]{2,1,0:T(8,128)} %param.10) | copy-start | bytes 1572868
  53.0 16.7 %copy-start = (f32[8,8,16,1024]{3,2,1,0:T(8,128)}, f32[8,8,16,1024]{3,2,1,0:T(8,128)S(1)}, u32[]{:S(2)}) copy-start(f32[8,8,16,1024]{3,2,1,0:T(8,128)S(1)} %get-tuple-element.10) | copy-start | bytes 12582916
  53.0 13.1 %slice-start = ((s8[12582912]{0:T(1024)(128)(4,1)}), s8[4194304]{0:T(1024)(128)(4,1)S(1)}, s32[]{:S(2)}) async-start(s8[12582912]{0:T(1024)(128)(4,1)} %bitcast.97), calls=%async_computation.1 | async-start | bytes 8388608
  53.2 13.0 %slice-start.1 = ((s8[12582912]{0:T(1024)(128)(4,1)}), s8[4194304]{0:T(1024)(128)(4,1)S(1)}, s32[]{:S(2)}) async-start(s8[12582912]{0:T(1024)(128)(4,1)} %bitcast.97), calls=%async_computation.2 | async-start | bytes 8388608
  53.2 13.0 %slice-start.2 = ((s8[12582912]{0:T(1024)(128)(4,1)}), s8[4194304]{0:T(1024)(128)(4,1)S(1)}, s32[]{:S(2)}) async-start(s8[12582912]{0:T(1024)(128)(4,1)} %bitcast.97), calls=%async_computation.3 | async-start | bytes 8388608
  58.2 11.4 %collective-permute-start.2 = (f32[9,1,16,1024]{3,2,1,0:T(8,128)S(1)}, f32[9,1,16,1024]{3,2,1,0:T(8,128)S(1)}, u32[]{:S(2)}, u32[]{:S(2)}) collective-permute-start(f32[9,1,16,1024]{3,2,1,0:T(8,128)S(1)} %get-tuple-element.27), channel_id=1, source_target_pairs={{1,0},{2,1},{3,2},{4,3},{5,4},{6,5},{7,6},{8,7},{9,8},{10,9},{11,1... | collective-permute-start | bytes 1769480 | tf_op jit(solution)/shard_map/ppermute | solution.py:30
  59.8 9.9 %collective-permute-start.3 = (f32[9,1,16,1024]{3,2,1,0:T(8,128)S(1)}, f32[9,1,16,1024]{3,2,1,0:T(8,128)S(1)}, u32[]{:S(2)}, u32[]{:S(2)}) collective-permute-start(f32[9,1,16,1024]{3,2,1,0:T(8,128)S(1)} %get-tuple-element.26), channel_id=1, source_target_pairs={{0,1},{1,2},{2,3},{3,4},{4,5},{5,6},{6,7},{7,8},{8,9},{9,10},{10,1... | collective-permute-start | bytes 1769480 | tf_op jit(solution)/shard_map/ppermute | solution.py:28
  69.7 5.4 %copy-start.12 = (f32[9,1,16,1024]{3,2,1,0:T(8,128)}, f32[9,1,16,1024]{3,2,1,0:T(8,128)S(1)}, u32[]{:S(2)}) copy-start(f32[9,1,16,1024]{3,2,1,0:T(8,128)S(1)} %collective-permute-done.2) | copy-start | bytes 1769476
  69.7 0.8 copy-start.14
  93.2 7.9 %copy-start.1 = (f32[8,8,16,1024]{3,2,1,0:T(8,128)S(1)}, f32[8,8,16,1024]{3,2,1,0:T(8,128)}, u32[]{:S(2)}) copy-start(f32[8,8,16,1024]{3,2,1,0:T(8,128)} %copy-done) | copy-start | bytes 12582916
  93.2 9.4 %copy-start.6 = (f32[9,8,16,1024]{3,2,1,0:T(8,128)S(1)}, f32[9,8,16,1024]{3,2,1,0:T(8,128)}, u32[]{:S(2)}) copy-start(f32[9,8,16,1024]{3,2,1,0:T(8,128)} %get-tuple-element.14) | copy-start | bytes 14155780
  93.2 10.7 %copy-start.7 = (f32[9,8,16,1024]{3,2,1,0:T(8,128)S(1)}, f32[9,8,16,1024]{3,2,1,0:T(8,128)}, u32[]{:S(2)}) copy-start(f32[9,8,16,1024]{3,2,1,0:T(8,128)} %get-tuple-element.15) | copy-start | bytes 14155780
  93.2 10.7 %copy-start.8 = (f32[8,16,1024]{2,1,0:T(8,128)S(1)}, f32[8,16,1024]{2,1,0:T(8,128)}, u32[]{:S(2)}) copy-start(f32[8,16,1024]{2,1,0:T(8,128)} %multiply_add_fusion.1) | copy-start | bytes 1572868
  93.2 10.9 %copy-start.11 = (s32[8,16,1024]{2,1,0:T(8,128)S(1)}, s32[8,16,1024]{2,1,0:T(8,128)}, u32[]{:S(2)}) copy-start(s32[8,16,1024]{2,1,0:T(8,128)} %param.14) | copy-start | bytes 1572868
  146.6 27.1 %all-to-all-start = ((f32[16,16,128]{2,1,0:T(8,128)}), f32[16,16,128]{2,1,0:T(8,128)S(1)}, u32[]{:S(2)}, u32[]{:S(2)}) async-start(f32[16,16,128]{2,1,0:T(8,128)} %bitcast.18), calls=%async_computation | async-start | bytes 262144 | tf_op jit(solution)/shard_map/all_to_all | solution.py:135
where the time goes:
time: 175 us; the launch traced here: 174 us
  other arithmetic  97.6 us (56%)
  local copies, waits for them, and re-layouts  49.2 us (28%)
  starting transfers between devices  26.6 us (15%)
    another operation x3, other arithmetic, shards(): tangents_out = jnp.stack([tan_v, tan_h, tan_c], axis=1)  23.1 us
    add x1, other arithmetic, advance(): tan_v + TIME_STEP * (diffusion[1:] + ionic_gain * (gating * current_slope...  19.5 us
    add x1, local copies, waits for them, and re-layouts, advance(): tan_v + TIME_STEP * (diffusion[1:] + ionic_gain * (gating * current_slope...  18.4 us
    slice x1, local copies, waits for them, and re-layouts, spread(): y_padded[..., 1:-1, :, 2:] - 2.0 * centre + y_padded[..., 1:-1, :, :-2]  18.1 us
    concatenate x6, other arithmetic, shards(): stacked = jnp.concatenate([voltage[None], tan_v], axis=0)  15.8 us
    all_to_all x1, starting transfers between devices, shards(): lax.all_to_all(outgoing.reshape(tile_count, CAP, row_size), 'tx', split_a...  14.9 us
    add x1, other arithmetic, spread(): coef_xx * along_x + coef_yy * along_y + 0.5 * coef_xy * cross_xy  13.7 us
    ppermute x2, starting transfers between devices, padded_2(): lax.ppermute(tail, axis, [(i, (i + 1) % count) for i in range(ends)])  8.77 us
  transfers between devices with their start and end apart: 5, of which 0 were waited for; matrix products, arithmetic and copies ran while one was open for 17% of the time, Pallas kernels for 0%

commit v1 on v0

v1 whole, which is shorter than its diff:
```python
import functools

import jax
import jax.numpy as jnp
from jax import lax
from jax.experimental import pallas as pl
from jax.experimental.pallas import tpu as pltpu
from jax.sharding import PartitionSpec as P

CAP = 16
LANES = 128
MIB = 1 << 20

CENTRE = 0.7
DEPTH = 0.025


def rolled(x, shift, axis):
    return pltpu.roll(x, shift % x.shape[axis], axis)


def stencil_coeffs(fiber):
    width = fiber.shape[-1]
    x_coef = jnp.where(fiber == 0, 0.1, jnp.where(fiber == 2, 0.025, 0.0625))
    y_coef = 0.125 - x_coef
    w_coef = jnp.where(fiber == 1, 0.01875, jnp.where(fiber == 3, -0.01875, 0.0))
    return (x_coef,) + shifted_pair(y_coef, width) + shifted_pair(w_coef, width)


def shifted_pair(coef, width):
    lane = lax.broadcasted_iota(jnp.int32, coef.shape, 1)
    before = jnp.where(lane == 0, 0.0, rolled(coef, 1, 1))
    after = jnp.where(lane == width - 1, 0.0, rolled(coef, -1, 1))
    return before, after


def depth_sum(u):
    level = lax.broadcasted_iota(jnp.int32, u.shape, 0)
    below = jnp.where(level == 0, u, rolled(u, 1, 0))
    above = jnp.where(level == u.shape[0] - 1, u, rolled(u, -1, 0))
    return below + above


def plane(u, low, high, coeffs):
    x_coef, y_before, y_after, w_before, w_after = coeffs
    if low is None:
        total, gap = high, high
    elif high is None:
        total, gap = low, -low
    else:
        total, gap = low + high, high - low
    return (
        x_coef * total
        + rolled(y_before * u + w_before * gap, -1, 1)
        + rolled(y_after * u - w_after * gap, 1, 1)
    )


def one_sided(u, sign, x_coef, w_before, w_after):
    part = rolled(w_before * u, -1, 1) - rolled(w_after * u, 1, 1)
    return x_coef * u + part if sign > 0 else x_coef * u - part


def local_gain(region, params):
    gain = jnp.zeros(region.shape, jnp.float32)
    for p in range(params.shape[0]):
        gain = jnp.where(region == p, params[p], gain)
    return 0.2 * gain


def reaction(v, h, gain):
    current = v - v * v * v * (1.0 / 3.0)
    slope = 1.0 - v * v
    gate = 1.0 / (1.0 + jnp.exp(-4.0 * v))
    of_v = CENTRE + gain * h * slope
    return of_v, gain * current, 0.2 * h * current, gate * (1.0 - gate), gate, gain * h * current


def edges_kernel(tan, v, left, right, sems):
    fields = tan.shape[0]
    last = tan.shape[2] - 1
    copies = []
    for k, (row, out) in enumerate(((0, left), (last, right))):
        copies.append(pltpu.make_async_copy(tan.at[:, 0, row], out.at[pl.ds(0, fields)], sems.at[2 * k]))
        copies.append(pltpu.make_async_copy(v.at[row], out.at[fields], sems.at[2 * k + 1]))
    for copy in copies:
        copy.start()
    for copy in copies:
        copy.wait()


def partial_kernel(params, *refs):
    ins, (left, right), coef = refs[:10], refs[10:12], refs[12]
    chunk = ins[0].shape[0]
    step = pl.program_id(0)
    for side, out in ((0, left), (1, right)):
        tan, v, h, reg, fib = ins[5 * side : 5 * side + 5]
        outer, inner = (0, 1) if side == 0 else (1, 0)

        @pl.when(step == 0)
        def _():
            fiber = fib[outer]
            of_v, of_h, of_m, _, _, _ = reaction(v[outer], h[outer], local_gain(reg[outer], params))
            for i, value in enumerate(stencil_coeffs(fiber) + (of_v, of_h, of_m)):
                coef[side, i] = value
            out[out.shape[0] - 1] = (fiber + 1).astype(jnp.float32)

        for j in range(chunk):
            p = step * chunk + j
            u, other = tan[j, 0, outer], tan[j, 0, inner]
            coeffs = tuple(coef[side, i] for i in range(5))
            low, high = (None, other) if side == 0 else (other, None)
            out[p] = (
                coef[side, 5] * u
                + plane(u, low, high, coeffs)
                + DEPTH * depth_sum(u)
                + coef[side, 6] * tan[j, 1, outer]
                + jnp.where(reg[outer] == p, coef[side, 7], 0.0)
                - 0.1 * tan[j, 2, outer]
            )


def main_kernel(params, v, h, c, reg, fib, tan, out, near, coef, gate_1, gate_2, dv, dh, dc):
    p = pl.program_id(0)
    rows = v.shape[0]

    def each_row(body):
        body(0, True, False)
        pl.loop(1, rows - 1)(lambda x: body(x, False, False))
        body(rows - 1, False, True)

    @pl.when(p == 0)
    def _():
        def base(x, first, last):
            coeffs = stencil_coeffs(fib[x])
            for i in range(5):
                coef[i, x] = coeffs[i]
            gain = local_gain(reg[x], params)
            u = v[x]
            of_v, of_h, of_m, of_g, gate, push = reaction(u, h[x], gain)
            for i, value in enumerate((of_v, of_h, of_m, of_g)):
                gate_1[i, x] = value
            low = None if first else v[x - 1]
            high = None if last else v[x + 1]
            u_new = CENTRE * u + plane(u, low, high, coeffs) + DEPTH * depth_sum(u) + push - 0.1 * c[x]
            h_new = 0.75 * h[x] + 0.25 * gate
            for i, value in enumerate(reaction(u_new, h_new, gain)[:4]):
                gate_2[i, x] = value

        each_row(base)

    def step_1(x, first, last):
        u = tan[0, 0, x]
        coeffs = tuple(coef[i, x] for i in range(5))
        low = None if first else tan[0, 0, x - 1]
        high = None if last else tan[0, 0, x + 1]
        dv[x] = (
            gate_1[0, x] * u
            + plane(u, low, high, coeffs)
            + DEPTH * depth_sum(u)
            + gate_1[1, x] * tan[0, 1, x]
            + jnp.where(reg[x] == p, gate_1[2, x], 0.0)
            - 0.1 * tan[0, 2, x]
        )
        new_h = 0.75 * tan[0, 1, x] + gate_1[3, x] * u
        new_c = 0.96 * tan[0, 2, x] + 0.05 * u
        if first or last:
            out[0, 1, x] = new_h
            out[0, 2, x] = new_c
        else:
            dh[x] = new_h
            dc[x] = new_c

    each_row(step_1)
    out[0, 0, 0] = dv[0]
    out[0, 0, rows - 1] = dv[rows - 1]
    near[0, 0] = dv[1]
    near[1, 0] = dv[rows - 2]

    def step_2(x):
        u = dv[x]
        coeffs = tuple(coef[i, x] for i in range(5))
        out[0, 0, x] = (
            gate_2[0, x] * u
            + plane(u, dv[x - 1], dv[x + 1], coeffs)
            + DEPTH * depth_sum(u)
            + gate_2[1, x] * dh[x]
            + jnp.where(reg[x] == p, gate_2[2, x], 0.0)
            - 0.1 * dc[x]
        )
        out[0, 1, x] = 0.75 * dh[x] + gate_2[3, x] * u
        out[0, 2, x] = 0.96 * dc[x] + 0.05 * u

    pl.loop(1, rows - 1)(step_2)


def tail_kernel(params, v, h, c, reg, fib, tan, near, al, al_v, ar, ar_v, bl, bl_f, br, br_f, part, out, coef):
    side_at, step = pl.program_id(0), pl.program_id(1)
    chunk = part.shape[0]

    def run(side, edge, edge_v, beyond, beyond_f):
        outer, inner = (0, 1) if side == 0 else (1, 0)
        sign = -1 if side == 0 else 1

        def ordered(outside, inside):
            return (outside, inside) if side == 0 else (inside, outside)

        @pl.when(step == 0)
        def _():
            coeffs = stencil_coeffs(fib[outer])
            gain = local_gain(reg[outer], params)
            u = v[outer]
            _, _, _, _, gate, push = reaction(u, h[outer], gain)
            low, high = ordered(edge_v[0], v[inner])
            u_new = CENTRE * u + plane(u, low, high, coeffs) + DEPTH * depth_sum(u) + push - 0.1 * c[outer]
            h_new = 0.75 * h[outer] + 0.25 * gate
            of_v, of_h, of_m, of_g, _, _ = reaction(u_new, h_new, gain)
            next_x, _, _, next_b, next_a = stencil_coeffs(fib[inner])
            sent = beyond_f[0]
            there = sent > 0.5
            far_x, _, _, far_b, far_a = stencil_coeffs((sent - 1.0).astype(jnp.int32))
            values = coeffs + (of_v, of_h, of_m, of_g, next_x, next_b, next_a)
            values = values + (jnp.where(there, far_x, 0.0), jnp.where(there, far_b, 0.0), jnp.where(there, far_a, 0.0))
            for i, value in enumerate(values):
                coef[i] = value

        for j in range(chunk):
            p = step * chunk + j
            coeffs = tuple(coef[i] for i in range(5))
            extra = one_sided(edge[j], sign, coeffs[0], coeffs[3], coeffs[4])
            u = part[j, 0, outer] + extra
            outside = beyond[j] + one_sided(tan[j, 0, 0], -sign, coef[12], coef[13], coef[14])
            low, high = ordered(outside, near[0, j])
            dh, dc = part[j, 1, outer], part[j, 2, outer]
            out[j, 0, outer] = (
                coef[5] * u
                + plane(u, low, high, coeffs)
                + DEPTH * depth_sum(u)
                + coef[6] * dh
                + jnp.where(reg[outer] == p, coef[7], 0.0)
                - 0.1 * dc
            )
            out[j, 1, outer] = 0.75 * dh + coef[8] * u
            out[j, 2, outer] = 0.96 * dc + 0.05 * u
            out[j, 0, inner] = part[j, 0, inner] + one_sided(extra, sign, coef[9], coef[10], coef[11])
            out[j, 1, inner] = part[j, 1, inner]
            out[j, 2, inner] = part[j, 2, inner]

    pl.when(side_at == 0)(lambda: run(0, al, al_v, bl, bl_f))
    pl.when(side_at == 1)(lambda: run(1, ar, ar_v, br, br_f))


def gather_kernel(sites, dv, out):
    fields, _, _, levels, width = dv.shape
    lane = lax.broadcasted_iota(jnp.int32, (LANES, LANES), 1)

    @pl.loop(0, out.shape[0] // LANES)
    def _(block):
        def take(k, acc):
            site = sites[block * LANES + k]
            held = jnp.maximum(site, 0)
            x, y = held // width, held % width
            start = pl.multiple_of((y // LANES) * LANES, LANES)
            found = dv[:, 0, x, :, pl.ds(start, LANES)].reshape(LANES, LANES)
            turn = (k - y % LANES + LANES) % LANES
            return jnp.where(lane == jnp.where(site < 0, -1, k), pltpu.roll(found, turn, 1), acc)

        acc = lax.fori_loop(0, LANES, take, jnp.zeros((LANES, LANES), jnp.float32), unroll=4)
        out[pl.ds(pl.multiple_of(block * LANES, LANES), LANES), :] = acc.T


def compiler_params(mib):
    return pltpu.CompilerParams(vmem_limit_bytes=mib * MIB)


def shards(voltage, gating, recovery, tangents, parameters, region, fiber_class, electrode_site, electrode_owner):
    rows, levels, width = voltage.shape
    fields = tangents.shape[0]
    tiles = lax.axis_size("tx")
    f32 = jnp.float32
    up = [(i, i + 1) for i in range(tiles - 1)]
    down = [(i + 1, i) for i in range(tiles - 1)]
    smem = pl.BlockSpec(memory_space=pltpu.SMEM)
    hbm = pl.BlockSpec(memory_space=pl.ANY)
    row = (levels, width)
    sent = jax.ShapeDtypeStruct((fields + 1,) + row, f32)

    edge_low, edge_high = pl.pallas_call(
        edges_kernel,
        out_shape=(sent, sent),
        in_specs=[hbm, hbm],
        out_specs=(hbm, hbm),
        scratch_shapes=[pltpu.SemaphoreType.DMA((4,))],
        name="edges",
    )(tangents, voltage)
    from_right = lax.ppermute(edge_low, "tx", down)
    from_left = lax.ppermute(edge_high, "tx", up)

    chunk = 2
    pairs = rows // 2

    def at(index):
        return lambda *grid: index(*grid)

    side_specs, side_args = [], []
    for side in range(2):
        place = 0 if side == 0 else pairs - 1
        side_specs.append(pl.BlockSpec((chunk, 3, 2) + row, functools.partial(lambda q, i: (i, 0, q, 0, 0), place)))
        side_args.append(tangents)
        for array in (voltage, gating, region, fiber_class):
            side_specs.append(pl.BlockSpec((2,) + row, functools.partial(lambda q, i: (q, 0, 0), place)))
            side_args.append(array)
    whole_sent = pl.BlockSpec((fields + 1,) + row, lambda i: (0, 0, 0))
    part_low, part_high = pl.pallas_call(
        partial_kernel,
        grid=(fields // chunk,),
        out_shape=(sent, sent),
        in_specs=[smem] + side_specs,
        out_specs=(whole_sent, whole_sent),
        scratch_shapes=[pltpu.VMEM((2, 8) + row, f32)],
        compiler_params=compiler_params(24),
        name="partial",
    )(parameters, *side_args)
    beyond_right = lax.ppermute(part_low, "tx", down)
    beyond_left = lax.ppermute(part_high, "tx", up)

    owners = electrode_owner[:, 0]
    count = owners.shape[0]
    order = jnp.arange(count, dtype=jnp.int32)
    same = (owners[:, None] == owners[None, :]) & (order[:, None] < order[None, :])
    target = owners * CAP + jnp.sum(same.astype(jnp.int32), axis=0)
    slots = jnp.arange(tiles * CAP, dtype=jnp.int32)
    sites = jnp.max(jnp.where(target[:, None] == slots[None, :], electrode_site[:, None], -1), axis=0)

    field = pl.BlockSpec((rows,) + row, lambda p: (0, 0, 0))
    tan_spec = pl.BlockSpec((1, 3, rows) + row, lambda p: (p, 0, 0, 0, 0))
    tile = (rows,) + row
    partial_out, near = pl.pallas_call(
        main_kernel,
        grid=(fields,),
        out_shape=(jax.ShapeDtypeStruct(tangents.shape, f32), jax.ShapeDtypeStruct((2, fields) + row, f32)),
        in_specs=[smem] + [field] * 5 + [tan_spec],
        out_specs=(tan_spec, pl.BlockSpec((2, 1) + row, lambda p: (0, p, 0, 0))),
        scratch_shapes=[
            pltpu.VMEM((5,) + tile, f32),
            pltpu.VMEM((4,) + tile, f32),
            pltpu.VMEM((4,) + tile, f32),
            pltpu.VMEM(tile, f32),
            pltpu.VMEM(tile, f32),
            pltpu.VMEM(tile, f32),
        ],
        compiler_params=compiler_params(32),
        cost_estimate=pl.CostEstimate(flops=200_000_000, bytes_accessed=28 * MIB, transcendentals=300_000),
        name="interior",
    )(parameters, voltage, gating, recovery, region, fiber_class, tangents)

    ends = pairs - 1
    base = pl.BlockSpec((2,) + row, lambda s, i: (s * ends, 0, 0))
    left = pl.BlockSpec((chunk,) + row, lambda s, i: (i * (1 - s) + (fields // chunk - 1) * s, 0, 0))
    right = pl.BlockSpec((chunk,) + row, lambda s, i: (i * s, 0, 0))
    extra = pl.BlockSpec((1,) + row, lambda s, i: (fields, 0, 0))
    pair = pl.BlockSpec((chunk, 3, 2) + row, lambda s, i: (i, 0, s * ends, 0, 0))
    tangents_out = pl.pallas_call(
        tail_kernel,
        grid=(2, fields // chunk),
        out_shape=jax.ShapeDtypeStruct(tangents.shape, f32),
        in_specs=[smem]
        + [base] * 5
        + [
            pl.BlockSpec((chunk, 1, 1) + row, lambda s, i: (i, 0, s * (rows - 1), 0, 0)),
            pl.BlockSpec((1, chunk) + row, lambda s, i: (s, i, 0, 0)),
            left,
            extra,
            right,
            extra,
            left,
            extra,
            right,
            extra,
            pair,
        ],
        out_specs=pair,
        scratch_shapes=[pltpu.VMEM((15,) + row, f32)],
        input_output_aliases={16: 0},
        compiler_params=compiler_params(24),
        name="tail",
    )(
        parameters,
        voltage,
        gating,
        recovery,
        region,
        fiber_class,
        tangents,
        near,
        from_left,
        from_left,
        from_right,
        from_right,
        beyond_left,
        beyond_left,
        beyond_right,
        beyond_right,
        partial_out,
    )

    outgoing = pl.pallas_call(
        gather_kernel,
        grid=(1,),
        out_shape=jax.ShapeDtypeStruct((tiles * CAP, fields * levels), f32),
        in_specs=[smem, pl.BlockSpec((fields, 1, rows) + row, lambda i: (0, 0, 0, 0, 0))],
        out_specs=pl.BlockSpec((tiles * CAP, fields * levels), lambda i: (0, 0)),
        compiler_params=compiler_params(24),
        name="gather",
    )(sites, tangents_out)
    arrived = lax.all_to_all(
        outgoing.reshape(tiles, CAP, fields * levels), "tx", split_axis=0, concat_axis=0, tiled=True
    )
    return tangents_out, arrived.reshape(tiles * CAP, fields * levels)


def solution(mesh):
    line = P(("groups", "tx"), None, None)
    placed = (
        line,
        line,
        line,
        P(None, None, ("groups", "tx"), None, None),
        P("groups"),
        line,
        line,
        P(("groups", "tx")),
        P(("groups", "tx"), None),
    )
    return jax.shard_map(
        shards,
        mesh=mesh,
        in_specs=placed,
        out_specs=(P(None, None, ("groups", "tx"), None, None), P(("groups", "tx"), None)),
        check_vma=False,
    )
```

time: 175 us -> 118 us (0.67)
  other arithmetic: 97.6 us -> 0.27 us
  Pallas kernels: 0 us -> 78.7 us
  local copies, waits for them, and re-layouts: 49.2 us -> 9.84 us
  blocking collectives: 0 us -> 16.9 us
  starting transfers between devices: 26.6 us -> 10.4 us
    pallas_call x0 -> x5, Pallas kernels: none -> 78.7 us  [the longest x1 36.9 us: shards(): pl.pallas_call(edges_kernel, out_shape=(sent, sent), in_specs=[hbm, hbm],...]
    add x4 -> x1, other arithmetic: 36.1 us -> 0.01 us  [shards(): target = owners * CAP + jnp.sum(same.astype(jnp.int32), axis=0)]
    concatenate x9 -> x0, other arithmetic: 24.3 us -> none  [the longest x6 15.8 us: shards(): stacked = jnp.concatenate([voltage[None], tan_v], axis=0)]
    another operation x5 -> x0, other arithmetic: 23.8 us -> none  [the longest x3 23.1 us: shards(): tangents_out = jnp.stack([tan_v, tan_h, tan_c], axis=1)]
    add x1 -> x0, local copies, waits for them, and re-layouts: 18.4 us -> none  [advance(): tan_v + TIME_STEP * (diffusion[1:] + ionic_gain * (gating * current_slope...]
    slice x2 -> x0, local copies, waits for them, and re-layouts: 18.3 us -> none  [the longest x1 18.1 us: spread(): y_padded[..., 1:-1, :, 2:] - 2.0 * centre + y_padded[..., 1:-1, :, :-2]]
    all_to_all x0 -> x1, blocking collectives: none -> 16.9 us  [shards(): lax.all_to_all(outgoing.reshape(tiles, CAP, fields * levels), 'tx', split...]
    all_to_all x1 -> x0, starting transfers between devices: 14.9 us -> none  [shards(): lax.all_to_all(outgoing.reshape(tile_count, CAP, row_size), 'tx', split_a...]
  transfers between devices with their start and end apart: 5 -> 4, of which waited for: 0 -> 0; matrix products, arithmetic and copies ran while one was open for 17% -> 0% of each run, Pallas kernels for 0% -> 19%
where the time goes in v1:
time: 118 us; the launch traced here: 117 us
  Pallas kernels  78.7 us (67%)
  blocking collectives  16.9 us (14%)
  starting transfers between devices  10.4 us (9%)
  local copies, waits for them, and re-layouts  9.84 us (8%)
    pallas_call x1, Pallas kernels, shards(): pl.pallas_call(edges_kernel, out_shape=(sent, sent), in_specs=[hbm, hbm],...  36.9 us
    pallas_call x1, Pallas kernels, shards(): pl.pallas_call(main_kernel, grid=(fields,), out_shape=(jax.ShapeDtypeStru...  19.3 us
    all_to_all x1, blocking collectives, shards(): lax.all_to_all(outgoing.reshape(tiles, CAP, fields * levels), 'tx', split...  16.9 us
    pallas_call x1, Pallas kernels, shards(): pl.pallas_call(gather_kernel, grid=(1,), out_shape=jax.ShapeDtypeStruct((...  10 us
    pallas_call x1, Pallas kernels, shards(): pl.pallas_call(tail_kernel, grid=(2, fields // chunk), out_shape=jax.Shap...  9.94 us
    unnamed x23, local copies, waits for them, and re-layouts  9.84 us
    ppermute x1, starting transfers between devices, shards(): beyond_left = lax.ppermute(part_high, 'tx', up)  5.43 us
    pallas_call x1, Pallas kernels, shards(): pl.pallas_call(partial_kernel, grid=(fields // chunk,), out_shape=(sent,...  2.62 us
  transfers between devices with their start and end apart: 4, of which 0 were waited for; matrix products, arithmetic and copies ran while one was open for 0% of the time, Pallas kernels for 19%

profile of v1, /device:TPU:0, one launch (start us, length us, event | category | flops | bytes accessed | tf_op | source)
XLA Modules:
  0.0 117.1 jit_solution(8062356002674940311)
XLA Ops:
  0.6 0.0 copy-start.3
  0.6 0.0 copy-start.4
  0.7 0.0 copy-start.8
  0.7 0.0 copy-start.5
  0.7 0.0 copy-start.6
  0.7 36.9 %edges.1 = (f32[9,16,1024]{2,1,0:T(8,128)}, f32[9,16,1024]{2,1,0:T(8,128)}) custom-call(f32[8,3,8,16,1024]{4,3,2,1,0:T(8,128)} %tan.5, f32[8,16,1024]{2,1,0:T(8,128)} %v.5), custom_call_target="tpu_custom_call" | custom-call | tf_op jit(solution)/shard_map/edges/pallas_call | solution.py:288
  37.6 2.4 %collective-permute-start = (f32[9,16,1024]{2,1,0:T(8,128)}, f32[9,16,1024]{2,1,0:T(8,128)S(1)}, u32[]{:S(2)}, u32[]{:S(2)}) collective-permute-start(f32[9,16,1024]{2,1,0:T(8,128)} %get-tuple-element.9), channel_id=1, source_target_pairs={{0,1},{1,2},{2,3},{3,4},{4,5},{5,6},{6,7},{7,8},{8,9},{9,10},{10,1... | collective-permute-start | bytes 1769480 | tf_op jit(solution)/shard_map/ppermute | solution.py:297
  40.0 1.3 %collective-permute-start.1 = (f32[9,16,1024]{2,1,0:T(8,128)}, f32[9,16,1024]{2,1,0:T(8,128)S(1)}, u32[]{:S(2)}, u32[]{:S(2)}) collective-permute-start(f32[9,16,1024]{2,1,0:T(8,128)} %get-tuple-element.10), channel_id=1, source_target_pairs={{1,0},{2,1},{3,2},{4,3},{5,4},{6,5},{7,6},{8,7},{9,8},{10,9},{11,1... | collective-permute-start | bytes 1769480 | tf_op jit(solution)/shard_map/ppermute | solution.py:296
  41.3 0.0 copy-done.3
  41.3 0.0 copy-done.4
  41.3 0.0 copy-start
  41.3 4.6 %copy-done = f32[8,3,8,16,1024]{4,3,2,1,0:T(8,128)S(1)} copy-done((f32[8,3,8,16,1024]{4,3,2,1,0:T(8,128)S(1)}, f32[8,3,8,16,1024]{4,3,2,1,0:T(8,128)}, u32[]{:S(2)}) %copy-start) | copy-done | bytes 12582936
  45.9 2.6 %partial.1 = (f32[9,16,1024]{2,1,0:T(8,128)S(1)}, f32[9,16,1024]{2,1,0:T(8,128)S(1)}) custom-call(f32[8]{0:T(128)S(1)} %copy-done.8, f32[8,3,8,16,1024]{4,3,2,1,0:T(8,128)S(1)} %copy-done, f32[8,16,1024]{2,1,0:T(8,128)S(1)} %copy-done.3, f32[8,16,1024]{2,1,0:T(8,128)S(1)} %copy-done.4, s32[8,16,1024]{2,1,0:T(8,128)S(1)} %copy-done.5, ...), custom_call_target="tpu_custom_call" | custom-call | tf_op jit(solution)/shard_map/partial/pallas_call | solution.py:314
  48.5 0.0 copy-start.9
  48.5 0.0 copy-start.10
  48.6 5.4 %collective-permute-start.2 = (f32[9,16,1024]{2,1,0:T(8,128)S(1)}, f32[9,16,1024]{2,1,0:T(8,128)S(1)}, u32[]{:S(2)}, u32[]{:S(2)}) collective-permute-start(f32[9,16,1024]{2,1,0:T(8,128)S(1)} %get-tuple-element.11), channel_id=1, source_target_pairs={{0,1},{1,2},{2,3},{3,4},{4,5},{5,6},{6,7},{7,8},{8,9},{9,10},{10,1... | collective-permute-start | bytes 1769480 | tf_op jit(solution)/shard_map/ppermute | solution.py:325
  54.0 1.3 %collective-permute-start.3 = (f32[9,16,1024]{2,1,0:T(8,128)S(1)}, f32[9,16,1024]{2,1,0:T(8,128)S(1)}, u32[]{:S(2)}, u32[]{:S(2)}) collective-permute-start(f32[9,16,1024]{2,1,0:T(8,128)S(1)} %get-tuple-element.12), channel_id=1, source_target_pairs={{1,0},{2,1},{3,2},{4,3},{5,4},{6,5},{7,6},{8,7},{9,8},{10,9},{11,1... | collective-permute-start | bytes 1769480 | tf_op jit(solution)/shard_map/ppermute | solution.py:324
  55.3 0.0 copy-done.1
  55.3 0.0 copy-done.7
  55.3 19.3 %interior.1 = (f32[8,3,8,16,1024]{4,3,2,1,0:T(8,128)}, f32[2,8,16,1024]{3,2,1,0:T(8,128)S(1)}) custom-call(f32[8]{0:T(128)S(1)} %copy-done.8, f32[8,16,1024]{2,1,0:T(8,128)S(1)} %copy-done.3, f32[8,16,1024]{2,1,0:T(8,128)S(1)} %copy-done.4, f32[8,16,1024]{2,1,0:T(8,128)S(1)} %copy-done.7, s32[8,16,1024]{2,1,0:T(8,128)S(1)} %copy-done.5, ...), custom_call_target="tpu_custom_call" | custom-call | flops 200000000 | bytes 29360128 | tf_op jit(solution)/shard_map/interior/pallas_call | solution.py:338
  74.6 0.0 copy-done.9
  74.6 0.1 convert_reduce_fusion
  74.7 0.1 select_reduce_fusion.sites
  74.9 0.0 collective-permute-done.al.al_v
  74.9 0.0 collective-permute-done.1.ar.ar_v
  74.9 0.0 collective-permute-done.2.bl.bl_f
  74.9 0.0 collective-permute-done.3.br.br_f
  74.9 9.9 %tail.1.dv = f32[8,3,8,16,1024]{4,3,2,1,0:T(8,128)} custom-call(f32[8]{0:T(128)S(1)} %copy-done.8, f32[8,16,1024]{2,1,0:T(8,128)S(1)} %copy-done.3, f32[8,16,1024]{2,1,0:T(8,128)S(1)} %copy-done.4, f32[8,16,1024]{2,1,0:T(8,128)S(1)} %copy-done.7, s32[8,16,1024]{2,1,0:T(8,128)S(1)} %copy-done.5, ...), custom_call_target="tpu_custom_call", output_to_operand_aliasing={{}: (16, {})} | custom-call | tf_op jit(solution)/shard_map/tail/pallas_call | solution.py:363
  84.9 4.6 %copy-done.2 = f32[8,3,8,16,1024]{4,3,2,1,0:T(8,128)S(1)} copy-done((f32[8,3,8,16,1024]{4,3,2,1,0:T(8,128)S(1)}, f32[8,3,8,16,1024]{4,3,2,1,0:T(8,128)}, u32[]{:S(2)}) %copy-start.2) | copy-done | bytes 12582936
  89.4 10.0 %gather.1 = f32[256,128]{1,0:T(8,128)S(1)} custom-call(s32[256]{0:T(256)S(1)} %select_reduce_fusion.sites, f32[8,3,8,16,1024]{4,3,2,1,0:T(8,128)S(1)} %copy-done.2), custom_call_target="tpu_custom_call" | custom-call | tf_op jit(solution)/shard_map/gather/pallas_call | solution.py:407
  99.5 16.9 %all_to_all.5 = f32[16,16,128]{2,1,0:T(8,128)S(1)} all-to-all(f32[16,16,128]{2,1,0:T(8,128)S(1)} %bitcast.5), channel_id=1, replica_groups=mesh['groups'=2,'tx'=16] {'tx'}, dimensions={0} | all-to-all | bytes 262144 | tf_op jit(solution)/shard_map/all_to_all | solution.py:416
  116.4 0.7 copy.14
  (8 shorter events, 0.0 us)
Async XLA Ops:
  0.6 40.6 %copy-start.3 = (f32[8,16,1024]{2,1,0:T(8,128)S(1)}, f32[8,16,1024]{2,1,0:T(8,128)}, u32[]{:S(2)}) copy-start(f32[8,16,1024]{2,1,0:T(8,128)} %v.5) | copy-start | bytes 1572868
  0.6 40.6 %copy-start.4 = (f32[8,16,1024]{2,1,0:T(8,128)S(1)}, f32[8,16,1024]{2,1,0:T(8,128)}, u32[]{:S(2)}) copy-start(f32[8,16,1024]{2,1,0:T(8,128)} %h.3) | copy-start | bytes 1572868
  0.7 40.6 %copy-start.8 = (f32[8]{0:T(128)S(1)}, f32[8]{0:T(128)}, u32[]{:S(2)}) copy-start(f32[8]{0:T(128)} %params.5) | copy-start | bytes 100
  0.7 40.6 %copy-start.5 = (s32[8,16,1024]{2,1,0:T(8,128)S(1)}, s32[8,16,1024]{2,1,0:T(8,128)}, u32[]{:S(2)}) copy-start(s32[8,16,1024]{2,1,0:T(8,128)} %reg.3) | copy-start | bytes 1572868
  0.7 40.6 %copy-start.6 = (s32[8,16,1024]{2,1,0:T(8,128)S(1)}, s32[8,16,1024]{2,1,0:T(8,128)}, u32[]{:S(2)}) copy-start(s32[8,16,1024]{2,1,0:T(8,128)} %fib.3) | copy-start | bytes 1572868
  37.6 37.3 %collective-permute-start = (f32[9,16,1024]{2,1,0:T(8,128)}, f32[9,16,1024]{2,1,0:T(8,128)S(1)}, u32[]{:S(2)}, u32[]{:S(2)}) collective-permute-start(f32[9,16,1024]{2,1,0:T(8,128)} %get-tuple-element.9), channel_id=1, source_target_pairs={{0,1},{1,2},{2,3},{3,4},{4,5},{5,6},{6,7},{7,8},{8,9},{9,10},{10,1... | collective-permute-start | bytes 1769480 | tf_op jit(solution)/shard_map/ppermute | solution.py:297
  40.0 34.9 %collective-permute-start.1 = (f32[9,16,1024]{2,1,0:T(8,128)}, f32[9,16,1024]{2,1,0:T(8,128)S(1)}, u32[]{:S(2)}, u32[]{:S(2)}) collective-permute-start(f32[9,16,1024]{2,1,0:T(8,128)} %get-tuple-element.10), channel_id=1, source_target_pairs={{1,0},{2,1},{3,2},{4,3},{5,4},{6,5},{7,6},{8,7},{9,8},{10,9},{11,1... | collective-permute-start | bytes 1769480 | tf_op jit(solution)/shard_map/ppermute | solution.py:296
  41.3 4.6 %copy-start = (f32[8,3,8,16,1024]{4,3,2,1,0:T(8,128)S(1)}, f32[8,3,8,16,1024]{4,3,2,1,0:T(8,128)}, u32[]{:S(2)}) copy-start(f32[8,3,8,16,1024]{4,3,2,1,0:T(8,128)} %tan.5) | copy-start | bytes 37748740
  45.9 9.4 %copy-start.1 = (f32[8,3,8,16,1024]{4,3,2,1,0:T(8,128)S(1)}, f32[8,3,8,16,1024]{4,3,2,1,0:T(8,128)}, u32[]{:S(2)}) copy-start(f32[8,3,8,16,1024]{4,3,2,1,0:T(8,128)} %tan.5) | copy-start | bytes 37748740
  45.9 9.4 %copy-start.7 = (f32[8,16,1024]{2,1,0:T(8,128)S(1)}, f32[8,16,1024]{2,1,0:T(8,128)}, u32[]{:S(2)}) copy-start(f32[8,16,1024]{2,1,0:T(8,128)} %c.3) | copy-start | bytes 1572868
  48.5 26.1 %copy-start.9 = (s32[256,1]{0,1:T(1,128)S(1)}, s32[256,1]{0,1:T(1,128)}, u32[]{:S(2)}) copy-start(s32[256,1]{0,1:T(1,128)} %param.17) | copy-start | bytes 3076
  48.5 26.2 %copy-start.10 = (s32[256]{0:T(256)S(1)}, s32[256]{0:T(256)}, u32[]{:S(2)}) copy-start(s32[256]{0:T(256)} %param.16) | copy-start | bytes 3076
  48.6 26.3 %collective-permute-start.2 = (f32[9,16,1024]{2,1,0:T(8,128)S(1)}, f32[9,16,1024]{2,1,0:T(8,128)S(1)}, u32[]{:S(2)}, u32[]{:S(2)}) collective-permute-start(f32[9,16,1024]{2,1,0:T(8,128)S(1)} %get-tuple-element.11), channel_id=1, source_target_pairs={{0,1},{1,2},{2,3},{3,4},{4,5},{5,6},{6,7},{7,8},{8,9},{9,10},{10,1... | collective-permute-start | bytes 1769480 | tf_op jit(solution)/shard_map/ppermute | solution.py:325
  54.0 20.9 %collective-permute-start.3 = (f32[9,16,1024]{2,1,0:T(8,128)S(1)}, f32[9,16,1024]{2,1,0:T(8,128)S(1)}, u32[]{:S(2)}, u32[]{:S(2)}) collective-permute-start(f32[9,16,1024]{2,1,0:T(8,128)S(1)} %get-tuple-element.12), channel_id=1, source_target_pairs={{1,0},{2,1},{3,2},{4,3},{5,4},{6,5},{7,6},{8,7},{9,8},{10,9},{11,1... | collective-permute-start | bytes 1769480 | tf_op jit(solution)/shard_map/ppermute | solution.py:324
  84.9 4.6 %copy-start.2 = (f32[8,3,8,16,1024]{4,3,2,1,0:T(8,128)S(1)}, f32[8,3,8,16,1024]{4,3,2,1,0:T(8,128)}, u32[]{:S(2)}) copy-start(f32[8,3,8,16,1024]{4,3,2,1,0:T(8,128)} %tail.1.dv) | copy-start | bytes 37748740

commit v2 on v0

v2 whole, which is shorter than its diff:
```python
import functools

import jax
import jax.numpy as jnp
from jax import lax
from jax.experimental import pallas as pl
from jax.experimental.pallas import tpu as pltpu
from jax.sharding import PartitionSpec as P

CAP = 16
GROUP = 8
LANES = 128
CHUNK = 2
MIB = 1 << 20

CENTRE = 0.7
DEPTH = 0.025


def rolled(x, shift, axis):
    return pltpu.roll(x, shift % x.shape[axis], axis)


def stencil_coeffs(fiber):
    width = fiber.shape[-1]
    x_coef = jnp.where(fiber == 0, 0.1, jnp.where(fiber == 2, 0.025, 0.0625))
    y_coef = 0.125 - x_coef
    w_coef = jnp.where(fiber == 1, 0.01875, jnp.where(fiber == 3, -0.01875, 0.0))
    return (x_coef,) + shifted_pair(y_coef, width) + shifted_pair(w_coef, width)


def shifted_pair(coef, width):
    lane = lax.broadcasted_iota(jnp.int32, coef.shape, 1)
    before = jnp.where(lane == 0, 0.0, rolled(coef, 1, 1))
    after = jnp.where(lane == width - 1, 0.0, rolled(coef, -1, 1))
    return before, after


def depth_sum(levels_of, k, count):
    u = levels_of(k)
    level = lax.broadcasted_iota(jnp.int32, u.shape, 0)
    first = u if k == 0 else rolled(levels_of(k - 1), 1, 0)
    last = u if k == count - 1 else rolled(levels_of(k + 1), -1, 0)
    return jnp.where(level == 0, first, rolled(u, 1, 0)) + jnp.where(level == GROUP - 1, last, rolled(u, -1, 0))


def plane(u, low, high, coeffs):
    x_coef, y_before, y_after, w_before, w_after = coeffs
    if low is None:
        total, gap = high, high
    elif high is None:
        total, gap = low, -low
    else:
        total, gap = low + high, high - low
    return (
        x_coef * total
        + rolled(y_before * u + w_before * gap, -1, 1)
        + rolled(y_after * u - w_after * gap, 1, 1)
    )


def one_sided(u, sign, x_coef, w_before, w_after):
    part = rolled(w_before * u, -1, 1) - rolled(w_after * u, 1, 1)
    return x_coef * u + part if sign > 0 else x_coef * u - part


def local_gain(region, params):
    gain = jnp.zeros(region.shape, jnp.float32)
    for p in range(params.shape[0]):
        gain = jnp.where(region == p, params[p], gain)
    return 0.2 * gain


def reaction(v, h, gain):
    current = v - v * v * v * (1.0 / 3.0)
    slope = 1.0 - v * v
    gate = 1.0 / (1.0 + jnp.exp(-4.0 * v))
    of_v = CENTRE + gain * h * slope
    return of_v, gain * current, 0.2 * h * current, gate * (1.0 - gate), gate, gain * h * current


def groups_of(levels):
    return [(k, pl.ds(GROUP * k, GROUP)) for k in range(levels // GROUP)]


def message_kernel(params, *refs):
    ins, (left, right), coef = refs[:10], refs[10:12], refs[12]
    chunk, fields = ins[0].shape[0], params.shape[0]
    groups = groups_of(ins[1].shape[1])
    step = pl.program_id(0)
    for side, out in ((0, left), (1, right)):
        tan, v, h, reg, fib = ins[5 * side : 5 * side + 5]
        outer, inner = (0, 1) if side == 0 else (1, 0)

        @pl.when(step == 0)
        def _():
            for _, z in groups:
                fiber = fib[outer, z]
                of_v, of_h, of_m, _, _, _ = reaction(v[outer, z], h[outer, z], local_gain(reg[outer, z], params))
                for i, value in enumerate(stencil_coeffs(fiber) + (of_v, of_h, of_m)):
                    coef[side, i, z] = value
                out[2 * fields, z] = v[outer, z]
                out[2 * fields + 1, z] = (fiber + 1).astype(jnp.float32)

        for j in range(chunk):
            p = step * chunk + j
            for k, z in groups:
                u, other = tan[j, 0, outer, z], tan[j, 0, inner, z]
                coeffs = tuple(coef[side, i, z] for i in range(5))
                low, high = (None, other) if side == 0 else (other, None)
                out[p, z] = u
                out[fields + p, z] = (
                    coef[side, 5, z] * u
                    + plane(u, low, high, coeffs)
                    + DEPTH * depth_sum(lambda i: tan[j, 0, outer, groups[i][1]], k, len(groups))
                    + coef[side, 6, z] * tan[j, 1, outer, z]
                    + jnp.where(reg[outer, z] == p, coef[side, 7, z], 0.0)
                    - 0.1 * tan[j, 2, outer, z]
                )


def main_kernel(params, v, h, c, reg, fib, tan, out, state, base_state, coef, gate_1, gate_2, dv, dh, dc):
    step = pl.program_id(0)
    rows, levels, _ = v.shape
    chunk = tan.shape[0]
    groups = groups_of(levels)

    def each_row(body):
        body(0, True, False)
        pl.loop(1, rows - 1)(lambda x: body(x, False, False))
        body(rows - 1, False, True)

    @pl.when(step == 0)
    def _():
        def base(x, first, last):
            for k, z in groups:
                coeffs = stencil_coeffs(fib[x, z])
                for i in range(5):
                    coef[i, x, z] = coeffs[i]
                gain = local_gain(reg[x, z], params)
                u = v[x, z]
                of_v, of_h, of_m, of_g, gate, push = reaction(u, h[x, z], gain)
                for i, value in enumerate((of_v, of_h, of_m, of_g)):
                    gate_1[i, x, z] = value
                low = None if first else v[x - 1, z]
                high = None if last else v[x + 1, z]
                depth = depth_sum(lambda i: v[x, groups[i][1]], k, len(groups))
                u_new = CENTRE * u + plane(u, low, high, coeffs) + DEPTH * depth + push - 0.1 * c[x, z]
                h_new = 0.75 * h[x, z] + 0.25 * gate
                if first or last:
                    values = coeffs + (u_new, h_new, gain, reg[x, z].astype(jnp.float32))
                    for i, value in enumerate(values):
                        base_state[int(last), i, z] = value
                else:
                    for i, value in enumerate(reaction(u_new, h_new, gain)[:4]):
                        gate_2[i, x, z] = value

        each_row(base)
        for side, x in ((0, 1), (1, rows - 2)):
            for i, at in enumerate((0, 3, 4)):
                base_state[side, 9 + i] = coef[at, x]

    def step_1(x, first, last):
        for k, z in groups:
            coeffs = tuple(coef[i, x, z] for i in range(5))
            for j in range(chunk):
                u = tan[j, 0, x, z]
                low = None if first else tan[j, 0, x - 1, z]
                high = None if last else tan[j, 0, x + 1, z]
                dv[j, x, z] = (
                    gate_1[0, x, z] * u
                    + plane(u, low, high, coeffs)
                    + DEPTH * depth_sum(lambda i: tan[j, 0, x, groups[i][1]], k, len(groups))
                    + gate_1[1, x, z] * tan[j, 1, x, z]
                    + jnp.where(reg[x, z] == step * chunk + j, gate_1[2, x, z], 0.0)
                    - 0.1 * tan[j, 2, x, z]
                )
                new_h = 0.75 * tan[j, 1, x, z] + gate_1[3, x, z] * u
                if first or last:
                    state[int(last), 0, j, z] = new_h
                    state[int(last), 1, j, z] = 0.096 * tan[j, 2, x, z] + 0.005 * u
                else:
                    dh[j, x, z] = new_h
                    dc[j, x, z] = 0.096 * tan[j, 2, x, z] + 0.005 * u

    each_row(step_1)

    def step_2(x):
        for k, z in groups:
            coeffs = tuple(coef[i, x, z] for i in range(5))
            for j in range(chunk):
                u = dv[j, x, z]
                out[j, 0, x, z] = (
                    gate_2[0, x, z] * u
                    + plane(u, dv[j, x - 1, z], dv[j, x + 1, z], coeffs)
                    + DEPTH * depth_sum(lambda i: dv[j, x, groups[i][1]], k, len(groups))
                    + gate_2[1, x, z] * dh[j, x, z]
                    + jnp.where(reg[x, z] == step * chunk + j, gate_2[2, x, z], 0.0)
                    - dc[j, x, z]
                )
                out[j, 1, x, z] = 0.75 * dh[j, x, z] + gate_2[3, x, z] * u
                out[j, 2, x, z] = 9.6 * dc[j, x, z] + 0.05 * u

    pl.loop(1, rows - 1)(step_2)
    for side, x in ((0, 1), (1, rows - 2)):
        for j in range(chunk):
            state[side, 2, j] = dv[j, x]
            state[side, 3, j] = out[j, 0, x]


def lay_columns(rows_of, laid, index):
    for at in range(laid.shape[1] // LANES):
        lanes = pl.ds(at * LANES, LANES)
        laid[index, lanes, :] = rows_of(lanes).reshape(LANES, LANES).T


def early_kernel(places, dv, out, laid):
    for at, x in enumerate(range(2, dv.shape[2] - 2)):
        lay_columns(lambda lanes: dv[:, 0, x, :, lanes], laid, at)
    width, count = laid.shape[1], laid.shape[0]
    flat = laid.reshape(count * width, laid.shape[2])

    def take(s, carry):
        place = places[s]
        out[pl.ds(s, 1), :] = jnp.where(place >= 0, flat[pl.ds(jnp.maximum(place, 0), 1), :], 0.0)
        return carry

    lax.fori_loop(0, out.shape[0], take, 0, unroll=8)


def tail_kernel(places, own_low, own_high, from_left, from_right, state, base_state, early, _, out, rows_out, dv, dh, dc, laid, coef, sems):
    fields, levels, width = dv.shape[2:]
    rows = out.shape[2]
    groups = groups_of(levels)
    copies = []
    for side, (own, there) in enumerate(((own_low, from_left), (own_high, from_right))):
        sign = -1 if side == 0 else 1

        def ordered(outside, inside):
            return (outside, inside) if side == 0 else (inside, outside)

        for k, z in groups:
            x_coef, y_before, y_after, w_before, w_after, v_new, h_new, gain = (base_state[side, i, z] for i in range(8))
            v_new = v_new + one_sided(there[2 * fields, z], sign, x_coef, w_before, w_after)
            for i, value in enumerate(reaction(v_new, h_new, gain)[:4]):
                coef[i, z] = value
            sent = there[2 * fields + 1, z]
            far = stencil_coeffs((sent - 1.0).astype(jnp.int32))
            for i, at in enumerate((0, 3, 4)):
                coef[4 + i, z] = jnp.where(sent > 0.5, far[at], 0.0)

        @pl.loop(0, fields)
        def _(p):
            for k, z in groups:
                x_coef, w_before, w_after = (base_state[side, i, z] for i in (0, 3, 4))
                extra = one_sided(there[p, z], sign, x_coef, w_before, w_after)
                dv[side, 0, p, z] = own[fields + p, z] + extra
                next_x, next_b, next_a = (base_state[side, 9 + i, z] for i in range(3))
                dv[side, 1, p, z] = state[side, 3, p, z] + one_sided(extra, sign, next_x, next_b, next_a)
            new = []
            for k, z in groups:
                u = dv[side, 0, p, z]
                outside = there[fields + p, z] + one_sided(own[p, z], -sign, coef[4, z], coef[5, z], coef[6, z])
                low, high = ordered(outside, state[side, 2, p, z])
                coeffs = tuple(base_state[side, i, z] for i in range(5))
                new.append(
                    coef[0, z] * u
                    + plane(u, low, high, coeffs)
                    + DEPTH * depth_sum(lambda i: dv[side, 0, p, groups[i][1]], k, len(groups))
                    + coef[1, z] * state[side, 0, p, z]
                    + jnp.where(base_state[side, 8, z] == p.astype(jnp.float32), coef[2, z], 0.0)
                    - state[side, 1, p, z]
                )
                dh[side, p, z] = 0.75 * state[side, 0, p, z] + coef[3, z] * u
                dc[side, p, z] = 9.6 * state[side, 1, p, z] + 0.05 * u
            for k, z in groups:
                dv[side, 0, p, z] = new[k]

        outer, inner = (0, 1) if side == 0 else (rows - 1, rows - 2)
        for i, (ref, target) in enumerate(
            (
                (dv.at[side, 0], out.at[:, 0, outer]),
                (dv.at[side, 1], out.at[:, 0, inner]),
                (dh.at[side], out.at[:, 1, outer]),
                (dc.at[side], out.at[:, 2, outer]),
            )
        ):
            copy = pltpu.make_async_copy(ref, target, sems.at[4 * side + i])
            copy.start()
            copies.append(copy)
        for i in range(2):
            lay_columns(lambda lanes: dv[side, i, :, :, lanes], laid, 2 * side + i)

    flat = laid.reshape(4 * width, laid.shape[2])

    def take(s, carry):
        place = places[s]
        line = pl.ds(s, 1)
        rows_out[line, :] = jnp.where(place >= 0, flat[pl.ds(jnp.maximum(place, 0), 1), :], early[line, :])
        return carry

    lax.fori_loop(0, rows_out.shape[0], take, 0, unroll=8)
    for copy in copies:
        copy.wait()


def compiler_params(mib):
    return pltpu.CompilerParams(vmem_limit_bytes=mib * MIB)


def shards(voltage, gating, recovery, tangents, parameters, region, fiber_class, electrode_site, electrode_owner):
    rows, levels, width = voltage.shape
    fields = tangents.shape[0]
    tiles = lax.axis_size("tx")
    f32 = jnp.float32
    up = [(i, i + 1) for i in range(tiles - 1)]
    down = [(i + 1, i) for i in range(tiles - 1)]
    smem = pl.BlockSpec(memory_space=pltpu.SMEM)
    hbm = pl.BlockSpec(memory_space=pl.ANY)
    vmem = pl.BlockSpec(memory_space=pltpu.VMEM)
    row = (levels, width)
    slots, depth = tiles * CAP, fields * levels
    message = jax.ShapeDtypeStruct((2 * fields + 2,) + row, f32)

    chunk = 2
    side_specs, side_args = [], []
    for side in range(2):
        place = 0 if side == 0 else rows // 2 - 1
        side_specs.append(pl.BlockSpec((chunk, 3, 2) + row, functools.partial(lambda q, i: (i, 0, q, 0, 0), place)))
        side_args.append(tangents)
        for array in (voltage, gating, region, fiber_class):
            side_specs.append(pl.BlockSpec((2,) + row, functools.partial(lambda q, i: (q, 0, 0), place)))
            side_args.append(array)
    whole = pl.BlockSpec(message.shape, lambda i: (0, 0, 0))
    own_low, own_high = pl.pallas_call(
        message_kernel,
        grid=(fields // chunk,),
        out_shape=(message, message),
        in_specs=[smem] + side_specs,
        out_specs=(whole, whole),
        scratch_shapes=[pltpu.VMEM((2, 8) + row, f32)],
        compiler_params=compiler_params(60),
        name="message",
    )(parameters, *side_args)
    from_right = lax.ppermute(own_low, "tx", down)
    from_left = lax.ppermute(own_high, "tx", up)

    owners = electrode_owner[:, 0]
    order = jnp.arange(owners.shape[0], dtype=jnp.int32)
    same = (owners[:, None] == owners[None, :]) & (order[:, None] < order[None, :])
    target = owners * CAP + jnp.sum(same.astype(jnp.int32), axis=0)
    sites = jnp.max(
        jnp.where(target[:, None] == jnp.arange(slots, dtype=jnp.int32)[None, :], electrode_site[:, None], -1), axis=0
    )
    site_x, site_y = sites // width, sites % width
    inside = (site_x >= 2) & (site_x < rows - 2) & (sites >= 0)
    early_places = jnp.where(inside, sites - 2 * width, -1)
    edge_row = jnp.where(site_x < 2, site_x, 2 + (rows - 1 - site_x))
    late_places = jnp.where(inside | (sites < 0), -1, edge_row * width + site_y)

    field = pl.BlockSpec((rows,) + row, lambda i: (0, 0, 0))
    tan_spec = pl.BlockSpec((CHUNK, 3, rows) + row, lambda i: (i, 0, 0, 0, 0))
    tile = (rows,) + row
    partial_out, state, base_state = pl.pallas_call(
        main_kernel,
        grid=(fields // CHUNK,),
        out_shape=(
            jax.ShapeDtypeStruct(tangents.shape, f32),
            jax.ShapeDtypeStruct((2, 4, fields) + row, f32),
            jax.ShapeDtypeStruct((2, 12) + row, f32),
        ),
        in_specs=[smem] + [field] * 5 + [tan_spec],
        out_specs=(
            tan_spec,
            pl.BlockSpec((2, 4, CHUNK) + row, lambda i: (0, 0, i, 0, 0)),
            pl.BlockSpec((2, 12) + row, lambda i: (0, 0, 0, 0)),
        ),
        scratch_shapes=[
            pltpu.VMEM((5,) + tile, f32),
            pltpu.VMEM((4,) + tile, f32),
            pltpu.VMEM((4,) + tile, f32),
            pltpu.VMEM((CHUNK,) + tile, f32),
            pltpu.VMEM((CHUNK,) + tile, f32),
            pltpu.VMEM((CHUNK,) + tile, f32),
        ],
        compiler_params=compiler_params(56),
        cost_estimate=pl.CostEstimate(flops=200_000_000, bytes_accessed=28 * MIB, transcendentals=300_000),
        name="interior",
    )(parameters, voltage, gating, recovery, region, fiber_class, tangents)

    early = pl.pallas_call(
        early_kernel,
        grid=(1,),
        out_shape=jax.ShapeDtypeStruct((slots, depth), f32),
        in_specs=[smem, pl.BlockSpec((fields, 1, rows) + row, lambda i: (0, 0, 0, 0, 0))],
        out_specs=pl.BlockSpec((slots, depth), lambda i: (0, 0)),
        scratch_shapes=[pltpu.VMEM((rows - 4, width, depth), f32)],
        compiler_params=compiler_params(56),
        cost_estimate=pl.CostEstimate(flops=20_000_000, bytes_accessed=12 * MIB, transcendentals=0),
        name="early",
    )(early_places, partial_out)

    tangents_out, outgoing = pl.pallas_call(
        tail_kernel,
        out_shape=(jax.ShapeDtypeStruct(tangents.shape, f32), jax.ShapeDtypeStruct((slots, depth), f32)),
        in_specs=[smem] + [vmem] * 7 + [hbm],
        out_specs=(hbm, vmem),
        scratch_shapes=[
            pltpu.VMEM((2, 2, fields) + row, f32),
            pltpu.VMEM((2, fields) + row, f32),
            pltpu.VMEM((2, fields) + row, f32),
            pltpu.VMEM((4, width, depth), f32),
            pltpu.VMEM((7,) + row, f32),
            pltpu.SemaphoreType.DMA((8,)),
        ],
        input_output_aliases={8: 0},
        compiler_params=compiler_params(32),
        name="tail",
    )(late_places, own_low, own_high, from_left, from_right, state, base_state, early, partial_out)

    arrived = lax.all_to_all(outgoing.reshape(tiles, CAP, depth), "tx", split_axis=0, concat_axis=0, tiled=True)
    return tangents_out, arrived.reshape(slots, depth)


def solution(mesh):
    line = P(("groups", "tx"), None, None)
    placed = (
        line,
        line,
        line,
        P(None, None, ("groups", "tx"), None, None),
        P("groups"),
        line,
        line,
        P(("groups", "tx")),
        P(("groups", "tx"), None),
    )
    return jax.shard_map(
        shards,
        mesh=mesh,
        in_specs=placed,
        out_specs=(P(None, None, ("groups", "tx"), None, None), P(("groups", "tx"), None)),
        check_vma=False,
    )
```

time: 175 us -> 62.4 us (0.36)
  other arithmetic: 97.6 us -> 0.88 us
  local copies, waits for them, and re-layouts: 49.2 us -> 1.79 us
  Pallas kernels: 0 us -> 37.1 us
  starting transfers between devices: 26.6 us -> 5.43 us
  blocking collectives: 0 us -> 16.1 us
    pallas_call x0 -> x4, Pallas kernels: none -> 37.1 us  [the longest x1 18.4 us: shards(): pl.pallas_call(main_kernel, grid=(fields // CHUNK,), out_shape=(jax.Shape...]
    add x4 -> x1, other arithmetic: 36.1 us -> 0.01 us  [shards(): target = owners * CAP + jnp.sum(same.astype(jnp.int32), axis=0)]
    concatenate x9 -> x0, other arithmetic: 24.3 us -> none  [the longest x6 15.8 us: shards(): stacked = jnp.concatenate([voltage[None], tan_v], axis=0)]
    another operation x5 -> x0, other arithmetic: 23.8 us -> none  [the longest x3 23.1 us: shards(): tangents_out = jnp.stack([tan_v, tan_h, tan_c], axis=1)]
    add x1 -> x0, local copies, waits for them, and re-layouts: 18.4 us -> none  [advance(): tan_v + TIME_STEP * (diffusion[1:] + ionic_gain * (gating * current_slope...]
    slice x2 -> x0, local copies, waits for them, and re-layouts: 18.3 us -> none  [the longest x1 18.1 us: spread(): y_padded[..., 1:-1, :, 2:] - 2.0 * centre + y_padded[..., 1:-1, :, :-2]]
    all_to_all x0 -> x1, blocking collectives: none -> 16.1 us  [shards(): lax.all_to_all(outgoing.reshape(tiles, CAP, depth), 'tx', split_axis=0, c...]
    all_to_all x1 -> x0, starting transfers between devices: 14.9 us -> none  [shards(): lax.all_to_all(outgoing.reshape(tile_count, CAP, row_size), 'tx', split_a...]
  transfers between devices with their start and end apart: 5 -> 2, of which waited for: 0 -> 0; matrix products, arithmetic and copies ran while one was open for 17% -> 1% of each run, Pallas kernels for 0% -> 37%
where the time goes in v2:
time: 62.4 us; the launch traced here: 62 us
  Pallas kernels  37.1 us (59%)
  blocking collectives  16.1 us (26%)
  starting transfers between devices  5.43 us (9%)
  local copies, waits for them, and re-layouts  1.79 us (3%)
  other arithmetic  0.88 us (1%)
  between operations  0.71 us (1%)
    pallas_call x1, Pallas kernels, shards(): pl.pallas_call(main_kernel, grid=(fields // CHUNK,), out_shape=(jax.Shape...  18.4 us
    all_to_all x1, blocking collectives, shards(): lax.all_to_all(outgoing.reshape(tiles, CAP, depth), 'tx', split_axis=0, c...  16.1 us
    pallas_call x1, Pallas kernels, shards(): pl.pallas_call(tail_kernel, out_shape=(jax.ShapeDtypeStruct(tangents.shap...  8.35 us
    pallas_call x1, Pallas kernels, shards(): pl.pallas_call(message_kernel, grid=(fields // chunk,), out_shape=(messag...  5.95 us
    pallas_call x1, Pallas kernels, shards(): pl.pallas_call(early_kernel, grid=(1,), out_shape=jax.ShapeDtypeStruct((s...  4.34 us
    ppermute x1, starting transfers between devices, shards(): from_left = lax.ppermute(own_high, 'tx', up)  4.15 us
    unnamed x15, local copies, waits for them, and re-layouts  1.79 us
    ppermute x1, starting transfers between devices, shards(): from_right = lax.ppermute(own_low, 'tx', down)  1.28 us
  transfers between devices with their start and end apart: 2, of which 0 were waited for; matrix products, arithmetic and copies ran while one was open for 1% of the time, Pallas kernels for 37%

profile of v2, /device:TPU:0, one launch (start us, length us, event | category | flops | bytes accessed | tf_op | source)
XLA Modules:
  0.0 62.0 jit_solution(308312550539330176)
XLA Ops:
  0.6 6.0 %message.1 = (f32[18,16,1024]{2,1,0:T(8,128)}, f32[18,16,1024]{2,1,0:T(8,128)}) custom-call(f32[8]{0:T(128)} %params.3, f32[8,3,8,16,1024]{4,3,2,1,0:T(8,128)} %tan.1, f32[8,16,1024]{2,1,0:T(8,128)} %v.1, f32[8,16,1024]{2,1,0:T(8,128)} %h.1, s32[8,16,1024]{2,1,0:T(8,128)} %reg.1, s32[8,16,1024]{2,1,0:T(8,128)} %fib.1, f32[8,3,8,16,1024]{4,3,2,1,0:T(8,128)} %tan.1, ...), custom_call_target="tpu_custom_call" | custom-call | tf_op jit(solution)/shard_map/message/pallas_call | solution.py:335
  6.6 1.3 %collective-permute-start.1 = (f32[18,16,1024]{2,1,0:T(8,128)}, f32[18,16,1024]{2,1,0:T(8,128)}, u32[]{:S(2)}, u32[]{:S(2)}) collective-permute-start(f32[18,16,1024]{2,1,0:T(8,128)} %get-tuple-element.9.own_low), channel_id=1, source_target_pairs={{1,0},{2,1},{3,2},{4,3},{5,4},{6,5},{7,6},{8,7},{9,8},{10,9},{11,1... | collective-permute-start | bytes 3538952 | tf_op jit(solution)/shard_map/ppermute | solution.py:345
  7.9 0.0 copy-start.5
  7.9 0.0 copy-start.6
  7.9 4.2 %collective-permute-start = (f32[18,16,1024]{2,1,0:T(8,128)}, f32[18,16,1024]{2,1,0:T(8,128)}, u32[]{:S(2)}, u32[]{:S(2)}) collective-permute-start(f32[18,16,1024]{2,1,0:T(8,128)} %get-tuple-element.10.own_high), channel_id=1, source_target_pairs={{0,1},{1,2},{2,3},{3,4},{4,5},{5,6},{6,7},{7,8},{8,9},{9,10},{10,1... | collective-permute-start | bytes 3538952 | tf_op jit(solution)/shard_map/ppermute | solution.py:346
  12.0 18.4 %interior.1 = (f32[8,3,8,16,1024]{4,3,2,1,0:T(8,128)}, f32[2,4,8,16,1024]{4,3,2,1,0:T(8,128)}, f32[2,12,16,1024]{3,2,1,0:T(8,128)}) custom-call(f32[8]{0:T(128)} %params.3, f32[8,16,1024]{2,1,0:T(8,128)} %v.1, f32[8,16,1024]{2,1,0:T(8,128)} %h.1, f32[8,16,1024]{2,1,0:T(8,128)} %c.1, s32[8,16,1024]{2,1,0:T(8,128)} %reg.1, s32[8,16,1024]{2,1,0:T(8,128)} %fib.1, ...), custom_call_target="tpu_custom_call" | custom-call | flops 200000000 | bytes 29360128 | tf_op jit(solution)/shard_map/interior/pallas_call | solution.py:364
  30.5 0.0 copy-done.5
  30.5 0.1 convert_reduce_fusion
  30.6 0.0 copy-done.6
  30.6 0.1 select_reduce_fusion
  30.8 0.6 add_select_fusion
  31.4 0.0 copy-start
  31.4 0.0 copy-start.1
  31.4 0.0 copy-start.2
  31.4 0.0 copy-start.3
  31.4 4.3 %early.1 = f32[256,128]{1,0:T(8,128)} custom-call(s32[256]{0:T(256)} %get-tuple-element.16.places, f32[8,3,8,16,1024]{4,3,2,1,0:T(8,128)} %get-tuple-element.13.dv._), custom_call_target="tpu_custom_call" | custom-call | flops 20000000 | bytes 12582912 | tf_op jit(solution)/shard_map/early/pallas_call | solution.py:391
  35.7 0.0 collective-permute-done.1.from_right
  35.7 0.0 collective-permute-done.from_left
  35.7 0.0 copy-done
  35.7 0.0 copy-done.1
  35.7 0.0 copy-done.2
  35.8 0.2 copy-done.3
  36.0 0.0 copy-start.4
  36.0 0.9 %copy-done.4 = f32[256,128]{1,0:T(8,128)S(1)} copy-done((f32[256,128]{1,0:T(8,128)S(1)}, f32[256,128]{1,0:T(8,128)}, u32[]{:S(2)}) %copy-start.4) | copy-done | bytes 131096
  36.9 8.3 %tail.1 = (f32[8,3,8,16,1024]{4,3,2,1,0:T(8,128)}, f32[256,128]{1,0:T(8,128)S(1)}) custom-call(s32[256]{0:T(256)S(1)} %get-tuple-element.17.places, f32[18,16,1024]{2,1,0:T(8,128)S(1)} %copy-done.2, f32[18,16,1024]{2,1,0:T(8,128)S(1)} %copy-done.3, f32[18,16,1024]{2,1,0:T(8,128)} %collective-permute-done.from_left, ...), custom_call_target="tpu_custom_call", output_to_operand_aliasing={{0}: (8, {})} | custom-call | tf_op jit(solution)/shard_map/tail/pallas_call | solution.py:403
  45.2 16.1 %all_to_all.5 = f32[16,16,128]{2,1,0:T(8,128)S(1)} all-to-all(f32[16,16,128]{2,1,0:T(8,128)S(1)} %bitcast.5), channel_id=1, replica_groups=mesh['groups'=2,'tx'=16] {'tx'}, dimensions={0} | all-to-all | bytes 262144 | tf_op jit(solution)/shard_map/all_to_all | solution.py:421
  61.4 0.7 %copy.14 = f32[256,128]{1,0:T(8,128)} copy(f32[256,128]{1,0:T(8,128)S(1)} %bitcast.6) | data formatting | bytes 262144
  (1 shorter events, 0.0 us)
Async XLA Ops:
  6.6 29.1 %collective-permute-start.1 = (f32[18,16,1024]{2,1,0:T(8,128)}, f32[18,16,1024]{2,1,0:T(8,128)}, u32[]{:S(2)}, u32[]{:S(2)}) collective-permute-start(f32[18,16,1024]{2,1,0:T(8,128)} %get-tuple-element.9.own_low), channel_id=1, source_target_pairs={{1,0},{2,1},{3,2},{4,3},{5,4},{6,5},{7,6},{8,7},{9,8},{10,9},{11,1... | collective-permute-start | bytes 3538952 | tf_op jit(solution)/shard_map/ppermute | solution.py:345
  7.9 22.6 %copy-start.5 = (s32[256,1]{0,1:T(1,128)S(1)}, s32[256,1]{0,1:T(1,128)}, u32[]{:S(2)}) copy-start(s32[256,1]{0,1:T(1,128)} %param.17) | copy-start | bytes 3076
  7.9 22.7 %copy-start.6 = (s32[256]{0:T(256)S(1)}, s32[256]{0:T(256)}, u32[]{:S(2)}) copy-start(s32[256]{0:T(256)} %param.16) | copy-start | bytes 3076
  7.9 27.8 %collective-permute-start = (f32[18,16,1024]{2,1,0:T(8,128)}, f32[18,16,1024]{2,1,0:T(8,128)}, u32[]{:S(2)}, u32[]{:S(2)}) collective-permute-start(f32[18,16,1024]{2,1,0:T(8,128)} %get-tuple-element.10.own_high), channel_id=1, source_target_pairs={{0,1},{1,2},{2,3},{3,4},{4,5},{5,6},{6,7},{7,8},{8,9},{9,10},{10,1... | collective-permute-start | bytes 3538952 | tf_op jit(solution)/shard_map/ppermute | solution.py:346
  31.4 4.4 %copy-start = (f32[2,4,8,16,1024]{4,3,2,1,0:T(8,128)S(1)}, f32[2,4,8,16,1024]{4,3,2,1,0:T(8,128)}, u32[]{:S(2)}) copy-start(f32[2,4,8,16,1024]{4,3,2,1,0:T(8,128)} %get-tuple-element.11.state) | copy-start | bytes 12582916
  31.4 4.4 %copy-start.1 = (f32[2,12,16,1024]{3,2,1,0:T(8,128)S(1)}, f32[2,12,16,1024]{3,2,1,0:T(8,128)}, u32[]{:S(2)}) copy-start(f32[2,12,16,1024]{3,2,1,0:T(8,128)} %get-tuple-element.12.base_state) | copy-start | bytes 4718596
  31.4 4.4 %copy-start.2 = (f32[18,16,1024]{2,1,0:T(8,128)S(1)}, f32[18,16,1024]{2,1,0:T(8,128)}, u32[]{:S(2)}) copy-start(f32[18,16,1024]{2,1,0:T(8,128)} %get-tuple-element.9.own_low) | copy-start | bytes 3538948
  31.4 4.6 %copy-start.3 = (f32[18,16,1024]{2,1,0:T(8,128)S(1)}, f32[18,16,1024]{2,1,0:T(8,128)}, u32[]{:S(2)}) copy-start(f32[18,16,1024]{2,1,0:T(8,128)} %get-tuple-element.10.own_high) | copy-start | bytes 3538948
  36.0 0.9 %copy-start.4 = (f32[256,128]{1,0:T(8,128)S(1)}, f32[256,128]{1,0:T(8,128)}, u32[]{:S(2)}) copy-start(f32[256,128]{1,0:T(8,128)} %early.1) | copy-start | bytes 393220

commit v3 on v2

v3 whole, which is shorter than its diff:
```python
import functools

import jax
import jax.numpy as jnp
from jax import lax
from jax.experimental import pallas as pl
from jax.experimental.pallas import tpu as pltpu
from jax.sharding import PartitionSpec as P

CAP = 16
GROUP = 8
LANES = 128
CHUNK = 2
MESSAGE_MIB = 54
MIB = 1 << 20

CENTRE = 0.7
DEPTH = 0.025


def rolled(x, shift, axis):
    return pltpu.roll(x, shift % x.shape[axis], axis)


def stencil_coeffs(fiber):
    width = fiber.shape[-1]
    x_coef = jnp.where(fiber == 0, 0.1, jnp.where(fiber == 2, 0.025, 0.0625))
    y_coef = 0.125 - x_coef
    w_coef = jnp.where(fiber == 1, 0.01875, jnp.where(fiber == 3, -0.01875, 0.0))
    return (x_coef,) + shifted_pair(y_coef, width) + shifted_pair(w_coef, width)


def shifted_pair(coef, width):
    lane = lax.broadcasted_iota(jnp.int32, coef.shape, 1)
    before = jnp.where(lane == 0, 0.0, rolled(coef, 1, 1))
    after = jnp.where(lane == width - 1, 0.0, rolled(coef, -1, 1))
    return before, after


def depth_sum(levels_of, k, count):
    u = levels_of(k)
    level = lax.broadcasted_iota(jnp.int32, u.shape, 0)
    first = u if k == 0 else rolled(levels_of(k - 1), 1, 0)
    last = u if k == count - 1 else rolled(levels_of(k + 1), -1, 0)
    return jnp.where(level == 0, first, rolled(u, 1, 0)) + jnp.where(level == GROUP - 1, last, rolled(u, -1, 0))


def plane(u, outside, inside, coeffs):
    x_coef, y_before, y_after, w_before, w_after = coeffs
    if outside is None:
        total, gap = inside, -inside
    else:
        total, gap = outside + inside, outside - inside
    return (
        x_coef * total
        + rolled(y_before * u + w_before * gap, -1, 1)
        + rolled(y_after * u - w_after * gap, 1, 1)
    )


def one_sided(u, x_coef, w_before, w_after):
    return x_coef * u + rolled(w_before * u, -1, 1) - rolled(w_after * u, 1, 1)


def signed(coeffs, sign):
    x_coef, y_before, y_after, w_before, w_after = coeffs
    return x_coef, y_before, y_after, sign * w_before, sign * w_after


def local_gain(region, params):
    gain = jnp.zeros(region.shape, jnp.float32)
    for p in range(params.shape[0]):
        gain = jnp.where(region == p, params[p], gain)
    return 0.2 * gain


def reaction(v, h, gain):
    current = v - v * v * v * (1.0 / 3.0)
    slope = 1.0 - v * v
    gate = 1.0 / (1.0 + jnp.exp(-4.0 * v))
    of_v = CENTRE + gain * h * slope
    return of_v, gain * current, 0.2 * h * current, gate * (1.0 - gate), gate, gain * h * current


def groups_of(levels):
    return [(k, pl.ds(GROUP * k, GROUP)) for k in range(levels // GROUP)]


def edge_of(side, rows):
    return side * (rows - 1), 1 + side * (rows - 3), (2 * side - 1).astype(jnp.float32)


def message_kernel(side_at, params, tan, v, h, reg, fib, out, dv, dhc, base, label, coef, sems):
    fields, rows = tan.shape[0], tan.shape[2]
    groups = groups_of(tan.shape[3])
    outer, inner, sign = edge_of(side_at[0], rows)
    half = fields // 2
    pairs = [
        (v.at[outer], out.at[2 * fields]),
        (h.at[outer], base),
        (reg.at[outer], label.at[0]),
        (fib.at[outer], label.at[1]),
    ]
    for at in (0, half):
        part = pl.ds(at, half)
        pairs += [
            (tan.at[part, 0, outer], out.at[part]),
            (tan.at[part, 0, inner], dv.at[part]),
            (tan.at[part, 1, outer], dhc.at[0, part]),
            (tan.at[part, 2, outer], dhc.at[1, part]),
        ]
    copies = [pltpu.make_async_copy(a, b, sems.at[k]) for k, (a, b) in enumerate(pairs)]
    for copy in copies:
        copy.start()

    for copy in copies[:4]:
        copy.wait()
    for _, z in groups:
        fiber = label[1, z]
        gain = local_gain(label[0, z], params)
        of_v, of_h, of_m, _, _, _ = reaction(out[2 * fields, z], base[z], gain)
        for i, value in enumerate(signed(stencil_coeffs(fiber), sign) + (of_v, of_h, of_m)):
            coef[i, z] = value
        out[2 * fields + 1, z] = (fiber + 1).astype(jnp.float32)

    for at in range(2):
        for copy in copies[4 + 4 * at : 8 + 4 * at]:
            copy.wait()

        @pl.loop(at * half // CHUNK, (at + 1) * half // CHUNK)
        def _(step):
            for k, z in groups:
                coeffs = tuple(coef[i, z] for i in range(5))
                for j in range(CHUNK):
                    p = step * CHUNK + j
                    u = out[p, z]
                    out[fields + p, z] = (
                        coef[5, z] * u
                        + plane(u, None, dv[p, z], coeffs)
                        + DEPTH * depth_sum(lambda i: out[p, groups[i][1]], k, len(groups))
                        + coef[6, z] * dhc[0, p, z]
                        + jnp.where(label[0, z] == p, coef[7, z], 0.0)
                        - 0.1 * dhc[1, p, z]
                    )


def main_kernel(
    side_at, params, v, h, c, reg, fib, tan, edge, out, state, base_state, held, now, later, rest,
    coef, gate_1, gate_2, dv, dh, dc
):
    step = pl.program_id(0)
    rows, levels, _ = v.shape
    link_outer, _, _ = edge_of(1 - side_at[0], rows)
    chip_outer, chip_inner, _ = edge_of(side_at[0], rows)
    chunk = tan.shape[0]
    groups = groups_of(levels)
    ends = ((0, 0), (1, rows - 1))

    @pl.when(step == 0)
    def _():
        def base(x, low, high, side):
            for k, z in groups:
                coeffs = stencil_coeffs(fib[x, z])
                gain = local_gain(reg[x, z], params)
                u = v[x, z]
                of_v, of_h, of_m, of_g, gate, push = reaction(u, h[x, z], gain)
                if side is not None:
                    coeffs = signed(coeffs, 2.0 * side - 1.0)
                for i in range(5):
                    coef[i, x, z] = coeffs[i]
                for i, value in enumerate((of_v, of_h, of_m, of_g)):
                    gate_1[i, x, z] = value
                depth = depth_sum(lambda i: v[x, groups[i][1]], k, len(groups))
                around = plane(u, v[high, z] if side is None else None, v[low, z], coeffs)
                u_new = CENTRE * u + around + DEPTH * depth + push - 0.1 * c[x, z]
                h_new = 0.75 * h[x, z] + 0.25 * gate
                if side is None:
                    for i, value in enumerate(reaction(u_new, h_new, gain)[:4]):
                        gate_2[i, x, z] = value
                else:
                    values = coeffs + (u_new, h_new, gain, reg[x, z].astype(jnp.float32))
                    for i, value in enumerate(values):
                        base_state[side, i, z] = value

        pl.loop(1, rows - 1)(lambda x: base(x, x - 1, x + 1, None))
        base(0, 1, None, 0)
        base(rows - 1, rows - 2, None, 1)
        for side, x in ((0, 1), (1, rows - 2)):
            base_state[side, 9] = coef[0, x]
            base_state[side, 10] = (2.0 * side - 1.0) * coef[3, x]
            base_state[side, 11] = (2.0 * side - 1.0) * coef[4, x]
        rest[0] = v[chip_outer]
        rest[1] = (fib[chip_outer] + 1).astype(jnp.float32)

    for j in range(chunk):
        dv[j, link_outer] = edge[j]
    for k, z in groups:
        coeffs = tuple(coef[i, chip_outer, z] for i in range(5))
        for j in range(chunk):
            u = tan[j, 0, chip_outer, z]
            new = (
                gate_1[0, chip_outer, z] * u
                + plane(u, None, tan[j, 0, chip_inner, z], coeffs)
                + DEPTH * depth_sum(lambda i: tan[j, 0, chip_outer, groups[i][1]], k, len(groups))
                + gate_1[1, chip_outer, z] * tan[j, 1, chip_outer, z]
                + jnp.where(reg[chip_outer, z] == step * chunk + j, gate_1[2, chip_outer, z], 0.0)
                - 0.1 * tan[j, 2, chip_outer, z]
            )
            dv[j, chip_outer, z] = new
            now[j, z] = u
            later[j, z] = new
    for side, x in ends:
        for k, z in groups:
            for j in range(chunk):
                u = tan[j, 0, x, z]
                state[side, 0, j, z] = 0.75 * tan[j, 1, x, z] + gate_1[3, x, z] * u
                state[side, 1, j, z] = 0.096 * tan[j, 2, x, z] + 0.005 * u

    def step_1(x):
        for k, z in groups:
            coeffs = tuple(coef[i, x, z] for i in range(5))
            for j in range(chunk):
                u = tan[j, 0, x, z]
                dv[j, x, z] = (
                    gate_1[0, x, z] * u
                    + plane(u, tan[j, 0, x + 1, z], tan[j, 0, x - 1, z], coeffs)
                    + DEPTH * depth_sum(lambda i: tan[j, 0, x, groups[i][1]], k, len(groups))
                    + gate_1[1, x, z] * tan[j, 1, x, z]
                    + jnp.where(reg[x, z] == step * chunk + j, gate_1[2, x, z], 0.0)
                    - 0.1 * tan[j, 2, x, z]
                )
                dh[j, x, z] = 0.75 * tan[j, 1, x, z] + gate_1[3, x, z] * u
                dc[j, x, z] = 0.096 * tan[j, 2, x, z] + 0.005 * u

    pl.loop(1, rows - 1)(step_1)

    def step_2(x):
        for k, z in groups:
            coeffs = tuple(coef[i, x, z] for i in range(5))
            for j in range(chunk):
                u = dv[j, x, z]
                new = (
                    gate_2[0, x, z] * u
                    + plane(u, dv[j, x + 1, z], dv[j, x - 1, z], coeffs)
                    + DEPTH * depth_sum(lambda i: dv[j, x, groups[i][1]], k, len(groups))
                    + gate_2[1, x, z] * dh[j, x, z]
                    + jnp.where(reg[x, z] == step * chunk + j, gate_2[2, x, z], 0.0)
                    - dc[j, x, z]
                )
                out[j, 0, x, z] = new
                held[j, x - 1, z] = new
                out[j, 1, x, z] = 0.75 * dh[j, x, z] + gate_2[3, x, z] * u
                out[j, 2, x, z] = 9.6 * dc[j, x, z] + 0.05 * u

    pl.loop(1, rows - 1)(step_2)
    for side, x in ((0, 1), (1, rows - 2)):
        for j in range(chunk):
            state[side, 2, j] = dv[j, x]


def lay_columns(rows_of, laid, index):
    for at in range(laid.shape[1] // LANES):
        lanes = pl.ds(at * LANES, LANES)
        laid[index, lanes, :] = rows_of(lanes).reshape(LANES, LANES).T


def take_columns(sites, laid, out, first, other):
    count, width, depth = laid.shape
    flat = laid.reshape(count * width, depth)

    def take(s, carry):
        place = sites[s] - first * width
        here = (sites[s] >= 0) & (place >= 0) & (place < count * width)
        line = pl.ds(s, 1)
        out[line, :] = jnp.where(here, flat[pl.ds(jnp.where(here, place, 0), 1), :], other(line))
        return carry

    lax.fori_loop(0, out.shape[0], take, 0, unroll=8)


def tail_kernel(side_at, sites, state, base_state, held, _, *refs):
    out, lines, dv, dh, dc, laid, coef, sems = refs[-8:]
    fields, levels, width = dv.shape[1:]
    if len(refs) == 11:
        own, there, before = refs[:3]
        now, later = own.at[pl.ds(0, fields)], own.at[pl.ds(fields, fields)]
        far_now, far_later, far_rest = (there.at[pl.ds(i * fields, fields if i < 2 else 2)] for i in range(3))
    else:
        now, later, far_now, far_later, far_rest = refs[:5]
        before = None
    rows = out.shape[2]
    groups = groups_of(levels)
    side = side_at[0]
    outer, inner, sign = edge_of(side, rows)

    for _, z in groups:
        v_new = base_state[side, 5, z] + one_sided(far_rest[0, z], *(base_state[side, i, z] for i in (0, 3, 4)))
        for i, value in enumerate(reaction(v_new, base_state[side, 6, z], base_state[side, 7, z])[:4]):
            coef[i, z] = value
        sent = far_rest[1, z]
        far = signed(stencil_coeffs((sent - 1.0).astype(jnp.int32)), -sign)
        for i, at in enumerate((0, 3, 4)):
            coef[4 + i, z] = jnp.where(sent > 0.5, far[at], 0.0)

    @pl.loop(0, fields // CHUNK)
    def _(step):
        for k, z in groups:
            own_row = tuple(base_state[side, i, z] for i in (0, 3, 4))
            next_row = tuple(base_state[side, 9 + i, z] for i in range(3))
            for j in range(CHUNK):
                p = step * CHUNK + j
                extra = one_sided(far_now[p, z], *own_row)
                dv[0, p, z] = later[p, z] + extra
                dv[1, p, z] = held[p, inner - 1, z] + one_sided(extra, *next_row)
        for k, z in groups:
            coeffs = tuple(base_state[side, i, z] for i in range(5))
            far = tuple(coef[i, z] for i in (4, 5, 6))
            for j in range(CHUNK):
                p = step * CHUNK + j
                u = dv[0, p, z]
                outside = far_later[p, z] + one_sided(now[p, z], *far)
                dv[2, p, z] = (
                    coef[0, z] * u
                    + plane(u, outside, state[side, 2, p, z], coeffs)
                    + DEPTH * depth_sum(lambda i: dv[0, p, groups[i][1]], k, len(groups))
                    + coef[1, z] * state[side, 0, p, z]
                    + jnp.where(base_state[side, 8, z] == p.astype(jnp.float32), coef[2, z], 0.0)
                    - state[side, 1, p, z]
                )
                dh[p, z] = 0.75 * state[side, 0, p, z] + coef[3, z] * u
                dc[p, z] = 9.6 * state[side, 1, p, z] + 0.05 * u

    copies = [
        pltpu.make_async_copy(ref, target, sems.at[i])
        for i, (ref, target) in enumerate(
            (
                (dv.at[2], out.at[:, 0, outer]),
                (dv.at[1], out.at[:, 0, inner]),
                (dh, out.at[:, 1, outer]),
                (dc, out.at[:, 2, outer]),
            )
        )
    ]
    for copy in copies:
        copy.start()
    count = laid.shape[0]
    first = side * (rows - count)
    lay_columns(lambda lanes: dv[2, :, :, lanes], laid, outer - first)
    lay_columns(lambda lanes: dv[1, :, :, lanes], laid, inner - first)
    if before is None:
        for x in range(2, rows - 2):
            lay_columns(lambda lanes: held[:, x - 1, :, lanes], laid, x - first)
    take_columns(
        sites, laid, lines, first, lambda line: jnp.zeros_like(lines[line, :]) if before is None else before[line, :]
    )
    for copy in copies:
        copy.wait()


def compiler_params(mib):
    return pltpu.CompilerParams(vmem_limit_bytes=mib * MIB)


def swapped(message, first, tiles):
    pairs = [(i, i + 1) for i in range(first, tiles - 1, 2)]
    return lax.ppermute(message, "tx", pairs + [(b, a) for a, b in pairs])


def shards(voltage, gating, recovery, tangents, parameters, region, fiber_class, electrode_site, electrode_owner):
    rows, levels, width = voltage.shape
    fields = tangents.shape[0]
    tiles = lax.axis_size("tx")
    f32 = jnp.float32
    smem = pl.BlockSpec(memory_space=pltpu.SMEM)
    hbm = pl.BlockSpec(memory_space=pl.ANY)
    vmem = pl.BlockSpec(memory_space=pltpu.VMEM)
    row = (levels, width)
    slots, depth = tiles * CAP, fields * levels
    linked = (lax.axis_index("tx") % 2).astype(jnp.int32)
    link_side, chip_side = linked.reshape(1), (1 - linked).reshape(1)

    message = jax.ShapeDtypeStruct((2 * fields + 2,) + row, f32)
    over_link = pl.pallas_call(
        message_kernel,
        out_shape=message,
        in_specs=[smem, smem] + [hbm] * 5,
        out_specs=vmem,
        scratch_shapes=[
            pltpu.VMEM((fields,) + row, f32),
            pltpu.VMEM((2, fields) + row, f32),
            pltpu.VMEM(row, f32),
            pltpu.VMEM((2,) + row, jnp.int32),
            pltpu.VMEM((8,) + row, f32),
            pltpu.SemaphoreType.DMA((12,)),
        ],
        compiler_params=compiler_params(MESSAGE_MIB),
        cost_estimate=pl.CostEstimate(flops=1_000_000_000, bytes_accessed=MIB, transcendentals=0),
        name="message",
    )(link_side, parameters, tangents, voltage, gating, region, fiber_class)
    from_link = swapped(over_link, 1, tiles)

    owners = electrode_owner[:, 0]
    order = jnp.arange(owners.shape[0], dtype=jnp.int32)
    same = (owners[:, None] == owners[None, :]) & (order[:, None] < order[None, :])
    target = owners * CAP + jnp.sum(same.astype(jnp.int32), axis=0)
    sites = jnp.max(
        jnp.where(target[:, None] == jnp.arange(slots, dtype=jnp.int32)[None, :], electrode_site[:, None], -1), axis=0
    )

    field = pl.BlockSpec((rows,) + row, lambda i: (0, 0, 0))
    tan_spec = pl.BlockSpec((CHUNK, 3, rows) + row, lambda i: (i, 0, 0, 0, 0))
    edge_spec = pl.BlockSpec((CHUNK,) + row, lambda i: (fields // CHUNK + i, 0, 0))
    tile = (rows,) + row
    partial_out, state, base_state, held, now, later, rest = pl.pallas_call(
        main_kernel,
        grid=(fields // CHUNK,),
        out_shape=(
            jax.ShapeDtypeStruct(tangents.shape, f32),
            jax.ShapeDtypeStruct((2, 3, fields) + row, f32),
            jax.ShapeDtypeStruct((2, 12) + row, f32),
            jax.ShapeDtypeStruct((fields, rows - 2) + row, f32),
            jax.ShapeDtypeStruct((fields,) + row, f32),
            jax.ShapeDtypeStruct((fields,) + row, f32),
            jax.ShapeDtypeStruct((2,) + row, f32),
        ),
        in_specs=[smem, smem] + [field] * 5 + [tan_spec, edge_spec],
        out_specs=(
            tan_spec,
            pl.BlockSpec((2, 3, CHUNK) + row, lambda i: (0, 0, i, 0, 0)),
            pl.BlockSpec((2, 12) + row, lambda i: (0, 0, 0, 0)),
            pl.BlockSpec((CHUNK, rows - 2) + row, lambda i: (i, 0, 0, 0)),
            pl.BlockSpec((CHUNK,) + row, lambda i: (i, 0, 0)),
            pl.BlockSpec((CHUNK,) + row, lambda i: (i, 0, 0)),
            pl.BlockSpec((2,) + row, lambda i: (0, 0, 0)),
        ),
        scratch_shapes=[
            pltpu.VMEM((5,) + tile, f32),
            pltpu.VMEM((4,) + tile, f32),
            pltpu.VMEM((4,) + tile, f32),
            pltpu.VMEM((CHUNK,) + tile, f32),
            pltpu.VMEM((CHUNK,) + tile, f32),
            pltpu.VMEM((CHUNK,) + tile, f32),
        ],
        compiler_params=compiler_params(36),
        cost_estimate=pl.CostEstimate(flops=1000, bytes_accessed=1024, transcendentals=0),
        name="interior",
    )(chip_side, parameters, voltage, gating, recovery, region, fiber_class, tangents, over_link)
    from_chip = tuple(swapped(part, 0, tiles) for part in (now, later, rest))

    def tail(side_at, filled, *messages):
        return pl.pallas_call(
            tail_kernel,
            out_shape=(jax.ShapeDtypeStruct(tangents.shape, f32), jax.ShapeDtypeStruct((slots, depth), f32)),
            in_specs=[smem, smem] + [vmem] * 3 + [hbm] + [vmem] * len(messages),
            out_specs=(hbm, vmem),
            scratch_shapes=[
                pltpu.VMEM((3, fields) + row, f32),
                pltpu.VMEM((fields,) + row, f32),
                pltpu.VMEM((fields,) + row, f32),
                pltpu.VMEM((2 if len(messages) == 3 else rows - 2, width, depth), f32),
                pltpu.VMEM((7,) + row, f32),
                pltpu.SemaphoreType.DMA((4,)),
            ],
            input_output_aliases={5: 0},
            compiler_params=compiler_params(20),
            cost_estimate=pl.CostEstimate(flops=1000, bytes_accessed=1024, transcendentals=0),
            name="tail",
        )(side_at, sites, state, base_state, held, filled, *messages)

    filled, lines = tail(chip_side, partial_out, now, later, *from_chip)
    from_link, lines = lax.optimization_barrier((from_link, lines))
    tangents_out, outgoing = tail(link_side, filled, over_link, from_link, lines)

    arrived = lax.all_to_all(outgoing.reshape(tiles, CAP, depth), "tx", split_axis=0, concat_axis=0, tiled=True)
    return tangents_out, arrived.reshape(slots, depth)


def solution(mesh):
    line = P(("groups", "tx"), None, None)
    placed = (
        line,
        line,
        line,
        P(None, None, ("groups", "tx"), None, None),
        P("groups"),
        line,
        line,
        P(("groups", "tx")),
        P(("groups", "tx"), None),
    )
    return jax.shard_map(
        shards,
        mesh=mesh,
        in_specs=placed,
        out_specs=(P(None, None, ("groups", "tx"), None, None), P(("groups", "tx"), None)),
        check_vma=False,
    )
```

time: 62.4 us -> 55.1 us (0.88)
  Pallas kernels: 37.1 us -> 30.7 us
  blocking collectives: 16.1 us -> 12.9 us
  waiting for transfers between devices: 0.01 us -> 1.69 us
  local copies, waits for them, and re-layouts: 1.79 us -> 2.99 us
    pallas_call x3, Pallas kernels: 18.6 us -> 14.5 us  [the longest x2 10.6 us: tail(): pl.pallas_call(tail_kernel, out_shape=(jax.ShapeDtypeStruct(tangents.shap...]
    all_to_all x1, blocking collectives: 16.1 us -> 12.9 us  [shards(): lax.all_to_all(outgoing.reshape(tiles, CAP, depth), 'tx', split_axis=0, c...]
    pallas_call x1, Pallas kernels: 18.4 us -> 16.1 us  [shards(): pl.pallas_call(main_kernel, grid=(fields // CHUNK,), out_shape=(jax.Shape...]
    ppermute x2 -> x4, waiting for transfers between devices: 0.01 us -> 1.69 us  [swapped(): return lax.ppermute(message, 'tx', pairs + [(b, a) for a, b in pairs])]
    unnamed x15 -> x19, local copies, waits for them, and re-layouts: 1.79 us -> 2.99 us
    ppermute x2 -> x4, starting transfers between devices: 5.43 us -> 5.5 us  [swapped(): return lax.ppermute(message, 'tx', pairs + [(b, a) for a, b in pairs])]
  transfers between devices with their start and end apart: 2 -> 4, of which waited for: 0 -> 1; matrix products, arithmetic and copies ran while one was open for 1% -> 0% of each run, Pallas kernels for 37% -> 40%
where the time goes in v3:
time: 55.1 us; the launch traced here: 54.8 us
  Pallas kernels  30.7 us (56%)
  blocking collectives  12.9 us (23%)
  starting transfers between devices  5.5 us (10%)
  local copies, waits for them, and re-layouts  2.99 us (5%)
  waiting for transfers between devices  1.69 us (3%)
  between operations  0.79 us (1%)
    pallas_call x1, Pallas kernels, shards(): pl.pallas_call(main_kernel, grid=(fields // CHUNK,), out_shape=(jax.Shape...  16.1 us
    all_to_all x1, blocking collectives, shards(): lax.all_to_all(outgoing.reshape(tiles, CAP, depth), 'tx', split_axis=0, c...  12.9 us
    pallas_call x2, Pallas kernels, tail(): pl.pallas_call(tail_kernel, out_shape=(jax.ShapeDtypeStruct(tangents.shap...  10.6 us
    ppermute x4, starting transfers between devices, swapped(): return lax.ppermute(message, 'tx', pairs + [(b, a) for a, b in pairs])  5.5 us
    pallas_call x1, Pallas kernels, shards(): pl.pallas_call(message_kernel, out_shape=message, in_specs=[smem, smem] +...  3.89 us
    unnamed x19, local copies, waits for them, and re-layouts  2.99 us
    ppermute x4, waiting for transfers between devices, swapped(): return lax.ppermute(message, 'tx', pairs + [(b, a) for a, b in pairs])  1.69 us
  transfers between devices with their start and end apart: 4, of which 1 were waited for; matrix products, arithmetic and copies ran while one was open for 0% of the time, Pallas kernels for 40%

profile of v3, /device:TPU:0, one launch (start us, length us, event | category | flops | bytes accessed | tf_op | source)
XLA Modules:
  0.0 54.8 jit_solution(17973079226522441096)
XLA Ops:
  0.6 0.0 copy-start.1
  0.7 0.0 copy-start.2
  0.7 0.0 copy-start.3
  0.7 0.0 copy-start.4
  0.7 0.0 copy-start.6
  0.7 3.9 %message.1.edge.refs_0_ = f32[18,16,1024]{2,1,0:T(8,128)} custom-call(s32[1]{0:T(128)} %bitcast.side_at, f32[8]{0:T(128)} %params.3, f32[8,3,8,16,1024]{4,3,2,1,0:T(8,128)} %tan.3, f32[8,16,1024]{2,1,0:T(8,128)} %v.3, f32[8,16,1024]{2,1,0:T(8,128)} %h.3, s32[8,16,1024]{2,1,0:T(8,128)} %reg.3, s32[8,16,1024]{2,1,0:T(8,128)} %fib.3), custom_call_target="tpu_custom_call" | custom-call | flops 1000000000 | bytes 1048576 | tf_op jit(solution)/shard_map/message/pallas_call | solution.py:383
  4.6 0.7 %collective-permute-start.3 = (f32[18,16,1024]{2,1,0:T(8,128)}, f32[18,16,1024]{2,1,0:T(8,128)S(1)}, u32[]{:S(2)}, u32[]{:S(2)}) collective-permute-start(f32[18,16,1024]{2,1,0:T(8,128)} %message.1.edge.refs_0_), channel_id=1, source_target_pairs={{1,2},{3,4},{5,6},{7,8},{9,10},{11,12},{13,14},{2,1},{4,3},{6,5},{... | collective-permute-start | bytes 3538952 | tf_op jit(solution)/shard_map/ppermute | solution.py:366
  5.3 0.0 copy-done.1
  5.3 0.0 copy-done.2
  5.4 0.0 copy-done.3
  5.4 0.0 copy-done.4
  5.4 0.0 copy-done.6
  5.4 0.0 copy-start
  5.4 1.3 %copy-done = f32[18,16,1024]{2,1,0:T(8,128)S(1)} copy-done((f32[18,16,1024]{2,1,0:T(8,128)S(1)}, f32[18,16,1024]{2,1,0:T(8,128)}, u32[]{:S(2)}) %copy-start) | copy-done | bytes 1179672
  6.7 0.0 copy-start.5
  6.7 1.0 %copy-done.5 = f32[8,16,1024]{2,1,0:T(8,128)S(1)} copy-done((f32[8,16,1024]{2,1,0:T(8,128)S(1)}, f32[8,16,1024]{2,1,0:T(8,128)}, u32[]{:S(2)}) %copy-start.5) | copy-done | bytes 524312
  7.7 16.1 %interior.1 = (f32[8,3,8,16,1024]{4,3,2,1,0:T(8,128)}, f32[2,3,8,16,1024]{4,3,2,1,0:T(8,128)S(1)}, f32[2,12,16,1024]{3,2,1,0:T(8,128)S(1)}, f32[8,6,16,1024]{3,2...) custom-call(s32[1]{0:T(128)} %bitcast.4.side_at, ...), custom_call_target="tpu_custom_call" | custom-call | flops 1000 | bytes 1024 | tf_op jit(solution)/shard_map/interior/pallas_call | solution.py:414
  23.8 4.3 %collective-permute-start = (f32[8,16,1024]{2,1,0:T(8,128)S(1)}, f32[8,16,1024]{2,1,0:T(8,128)S(1)}, u32[]{:S(2)}, u32[]{:S(2)}) collective-permute-start(f32[8,16,1024]{2,1,0:T(8,128)S(1)} %get-tuple-element.19.refs_0_), channel_id=1, source_target_pairs={{0,1},{2,3},{4,5},{6,7},{8,9},{10,11},{12,13},{14,15},{1,0},{3,2},... | collective-permute-start | bytes 1572872 | tf_op jit(solution)/shard_map/ppermute | solution.py:366
  28.1 0.0 collective-permute-start.1
  28.1 0.5 collective-permute-start.2
  28.6 0.0 copy-done.7
  28.6 0.1 convert_reduce_fusion
  28.7 0.0 copy-done.8
  28.7 0.1 select_reduce_fusion.sites
  28.9 1.7 %collective-permute-done.2.refs_4_ = f32[2,16,1024]{2,1,0:T(8,128)S(1)} collective-permute-done((f32[2,16,1024]{2,1,0:T(8,128)S(1)}, f32[2,16,1024]{2,1,0:T(8,128)S(1)}, u32[]{:S(2)}, u32[]{:S(2)}) %collective-permute-start.2) | collective-permute-done | bytes 131104 | tf_op jit(solution)/shard_map/ppermute | solution.py:366
  30.6 0.0 collective-permute-done.refs_2_
  30.6 0.0 collective-permute-done.1.refs_3_
  30.6 5.6 %tail.2 = (f32[8,3,8,16,1024]{4,3,2,1,0:T(8,128)}, f32[256,128]{1,0:T(8,128)S(1)}) custom-call(s32[1]{0:T(128)} %bitcast.4.side_at, s32[256]{0:T(256)S(1)} %select_reduce_fusion.sites, f32[2,3,8,16,1024]{4,3,2,1,0:T(8,128)S(1)} %get-tuple-element.15.state, f32[2,12,16,1024]{3,2,1,0:T(8,128)S(1)} %get-tuple-element.16.base_state, ...), custom_call_target="tpu_custom_call", output_to_operand_aliasing={{0}: (5, {})} | custom-call | flops 1000 | bytes 1024 | tf_op jit(solution)/shard_map/tail/pallas_call | solution.py:451
  36.2 0.0 collective-permute-done.3.refs_1_
  36.2 5.0 %tail.3 = (f32[8,3,8,16,1024]{4,3,2,1,0:T(8,128)}, f32[256,128]{1,0:T(8,128)S(1)}) custom-call(s32[1]{0:T(128)} %bitcast.side_at, s32[256]{0:T(256)S(1)} %select_reduce_fusion.sites, f32[2,3,8,16,1024]{4,3,2,1,0:T(8,128)S(1)} %get-tuple-element.15.state, f32[2,12,16,1024]{3,2,1,0:T(8,128)S(1)} %get-tuple-element.16.base_state, ...), custom_call_target="tpu_custom_call", output_to_operand_aliasing={{0}: (5, {})} | custom-call | flops 1000 | bytes 1024 | tf_op jit(solution)/shard_map/tail/pallas_call | solution.py:451
  41.2 12.9 %all_to_all.5 = f32[16,16,128]{2,1,0:T(8,128)S(1)} all-to-all(f32[16,16,128]{2,1,0:T(8,128)S(1)} %bitcast.7), channel_id=1, replica_groups=mesh['groups'=2,'tx'=16] {'tx'}, dimensions={0} | all-to-all | bytes 262144 | tf_op jit(solution)/shard_map/all_to_all | solution.py:474
  54.1 0.7 %copy.16 = f32[256,128]{1,0:T(8,128)} copy(f32[256,128]{1,0:T(8,128)S(1)} %bitcast.8) | data formatting | bytes 262144
  (3 shorter events, 0.0 us)
Async XLA Ops:
  0.6 4.7 %copy-start.1 = (f32[8,16,1024]{2,1,0:T(8,128)S(1)}, f32[8,16,1024]{2,1,0:T(8,128)}, u32[]{:S(2)}) copy-start(f32[8,16,1024]{2,1,0:T(8,128)} %v.3) | copy-start | bytes 1572868
  0.7 4.7 %copy-start.2 = (f32[8,16,1024]{2,1,0:T(8,128)S(1)}, f32[8,16,1024]{2,1,0:T(8,128)}, u32[]{:S(2)}) copy-start(f32[8,16,1024]{2,1,0:T(8,128)} %h.3) | copy-start | bytes 1572868
  0.7 4.7 %copy-start.3 = (s32[8,16,1024]{2,1,0:T(8,128)S(1)}, s32[8,16,1024]{2,1,0:T(8,128)}, u32[]{:S(2)}) copy-start(s32[8,16,1024]{2,1,0:T(8,128)} %reg.3) | copy-start | bytes 1572868
  0.7 4.7 %copy-start.4 = (s32[8,16,1024]{2,1,0:T(8,128)S(1)}, s32[8,16,1024]{2,1,0:T(8,128)}, u32[]{:S(2)}) copy-start(s32[8,16,1024]{2,1,0:T(8,128)} %fib.3) | copy-start | bytes 1572868
  0.7 4.7 %copy-start.6 = (f32[8]{0:T(128)S(1)}, f32[8]{0:T(128)}, u32[]{:S(2)}) copy-start(f32[8]{0:T(128)} %params.3) | copy-start | bytes 100
  4.6 31.6 %collective-permute-start.3 = (f32[18,16,1024]{2,1,0:T(8,128)}, f32[18,16,1024]{2,1,0:T(8,128)S(1)}, u32[]{:S(2)}, u32[]{:S(2)}) collective-permute-start(f32[18,16,1024]{2,1,0:T(8,128)} %message.1.edge.refs_0_), channel_id=1, source_target_pairs={{1,2},{3,4},{5,6},{7,8},{9,10},{11,12},{13,14},{2,1},{4,3},{6,5},{... | collective-permute-start | bytes 3538952 | tf_op jit(solution)/shard_map/ppermute | solution.py:366
  5.4 1.3 %copy-start = (f32[18,16,1024]{2,1,0:T(8,128)S(1)}, f32[18,16,1024]{2,1,0:T(8,128)}, u32[]{:S(2)}) copy-start(f32[18,16,1024]{2,1,0:T(8,128)} %message.1.edge.refs_0_) | copy-start | bytes 3538948
  6.7 1.0 %copy-start.5 = (f32[8,16,1024]{2,1,0:T(8,128)S(1)}, f32[8,16,1024]{2,1,0:T(8,128)}, u32[]{:S(2)}) copy-start(f32[8,16,1024]{2,1,0:T(8,128)} %c.1) | copy-start | bytes 1572868
  7.7 20.9 %copy-start.7 = (s32[256,1]{0,1:T(1,128)S(1)}, s32[256,1]{0,1:T(1,128)}, u32[]{:S(2)}) copy-start(s32[256,1]{0,1:T(1,128)} %param.17) | copy-start | bytes 3076
  7.7 21.0 %copy-start.8 = (s32[256]{0:T(256)S(1)}, s32[256]{0:T(256)}, u32[]{:S(2)}) copy-start(s32[256]{0:T(256)} %param.16) | copy-start | bytes 3076
  23.8 6.7 %collective-permute-start = (f32[8,16,1024]{2,1,0:T(8,128)S(1)}, f32[8,16,1024]{2,1,0:T(8,128)S(1)}, u32[]{:S(2)}, u32[]{:S(2)}) collective-permute-start(f32[8,16,1024]{2,1,0:T(8,128)S(1)} %get-tuple-element.19.refs_0_), channel_id=1, source_target_pairs={{0,1},{2,3},{4,5},{6,7},{8,9},{10,11},{12,13},{14,15},{1,0},{3,2},... | collective-permute-start | bytes 1572872 | tf_op jit(solution)/shard_map/ppermute | solution.py:366
  28.1 2.5 %collective-permute-start.1 = (f32[8,16,1024]{2,1,0:T(8,128)S(1)}, f32[8,16,1024]{2,1,0:T(8,128)S(1)}, u32[]{:S(2)}, u32[]{:S(2)}) collective-permute-start(f32[8,16,1024]{2,1,0:T(8,128)S(1)} %get-tuple-element.20.refs_1_), channel_id=1, source_target_pairs={{0,1},{2,3},{4,5},{6,7},{8,9},{10,11},{12,13},{14,15},{1,0},{3,2},... | collective-permute-start | bytes 1572872 | tf_op jit(solution)/shard_map/ppermute | solution.py:366
  28.1 2.5 %collective-permute-start.2 = (f32[2,16,1024]{2,1,0:T(8,128)S(1)}, f32[2,16,1024]{2,1,0:T(8,128)S(1)}, u32[]{:S(2)}, u32[]{:S(2)}) collective-permute-start(f32[2,16,1024]{2,1,0:T(8,128)S(1)} %get-tuple-element.21), channel_id=1, source_target_pairs={{0,1},{2,3},{4,5},{6,7},{8,9},{10,11},{12,13},{14,15},{1,0},{3,2},... | collective-permute-start | bytes 393224 | tf_op jit(solution)/shard_map/ppermute | solution.py:366

commit v4 on v3

--- a/solution.py
+++ b/solution.py
@@ -12,6 +12,7 @@
 LANES = 128
 CHUNK = 2
 MESSAGE_MIB = 54
+INTERIOR_MIB = 36
 MIB = 1 << 20
 
 CENTRE = 0.7
@@ -90,7 +91,7 @@
     return side * (rows - 1), 1 + side * (rows - 3), (2 * side - 1).astype(jnp.float32)
 
 
-def message_kernel(side_at, params, tan, v, h, reg, fib, out, dv, dhc, base, label, coef, sems):
+def message_kernel(side_at, params, tan, v, h, reg, fib, sent, out, dv, dhc, base, label, coef, sems, sent_sems):
     fields, rows = tan.shape[0], tan.shape[2]
     groups = groups_of(tan.shape[3])
     outer, inner, sign = edge_of(side_at[0], rows)
@@ -113,6 +114,10 @@
     for copy in copies:
         copy.start()
 
+    def send(first, count, k):
+        part = pl.ds(first, count)
+        return pltpu.make_async_copy(out.at[part], sent.at[part], sent_sems.at[k])
+
     for copy in copies[:4]:
         copy.wait()
     for _, z in groups:
@@ -122,10 +127,12 @@
         for i, value in enumerate(signed(stencil_coeffs(fiber), sign) + (of_v, of_h, of_m)):
             coef[i, z] = value
         out[2 * fields + 1, z] = (fiber + 1).astype(jnp.float32)
+    send(2 * fields, 2, 0).start()
 
     for at in range(2):
         for copy in copies[4 + 4 * at : 8 + 4 * at]:
             copy.wait()
+        send(at * half, half, 1 + at).start()
 
         @pl.loop(at * half // CHUNK, (at + 1) * half // CHUNK)
         def _(step):
@@ -142,19 +149,33 @@
                         + jnp.where(label[0, z] == p, coef[7, z], 0.0)
                         - 0.1 * dhc[1, p, z]
                     )
+            send(fields + step * CHUNK, CHUNK, 3).start()
+
+    send(2 * fields, 2, 0).wait()
+    for at in range(2):
+        send(at * half, half, 1 + at).wait()
+    send(fields, fields, 3).wait()
 
 
 def main_kernel(
-    side_at, params, v, h, c, reg, fib, tan, edge, out, state, base_state, held, now, later, rest,
-    coef, gate_1, gate_2, dv, dh, dc
+    side_at, params, v, h, c, reg, fib, tan_all, out, state, base_state, held, now, later, rest,
+    coef, gate_1, gate_2, dv, dh, dc, slots, sems
 ):
     step = pl.program_id(0)
     rows, levels, _ = v.shape
-    link_outer, _, _ = edge_of(1 - side_at[0], rows)
-    chip_outer, chip_inner, _ = edge_of(side_at[0], rows)
-    chunk = tan.shape[0]
+    chip_outer, _, _ = edge_of(side_at[0], rows)
+    chunk, count = CHUNK, pl.num_programs(0)
     groups = groups_of(levels)
     ends = ((0, 0), (1, rows - 1))
+    tan = slots.at[step % 2]
+
+    def load(at, slot):
+        return pltpu.make_async_copy(tan_all.at[pl.ds(at * chunk, chunk)], slots.at[slot], sems.at[slot])
+
+    @pl.when(step == 0)
+    def _():
+        for slot in range(2):
+            load(slot, slot).start()
 
     @pl.when(step == 0)
     def _():
@@ -192,29 +213,26 @@
         rest[0] = v[chip_outer]
         rest[1] = (fib[chip_outer] + 1).astype(jnp.float32)
 
-    for j in range(chunk):
-        dv[j, link_outer] = edge[j]
-    for k, z in groups:
-        coeffs = tuple(coef[i, chip_outer, z] for i in range(5))
-        for j in range(chunk):
-            u = tan[j, 0, chip_outer, z]
-            new = (
-                gate_1[0, chip_outer, z] * u
-                + plane(u, None, tan[j, 0, chip_inner, z], coeffs)
-                + DEPTH * depth_sum(lambda i: tan[j, 0, chip_outer, groups[i][1]], k, len(groups))
-                + gate_1[1, chip_outer, z] * tan[j, 1, chip_outer, z]
-                + jnp.where(reg[chip_outer, z] == step * chunk + j, gate_1[2, chip_outer, z], 0.0)
-                - 0.1 * tan[j, 2, chip_outer, z]
-            )
-            dv[j, chip_outer, z] = new
-            now[j, z] = u
-            later[j, z] = new
+    load(step, step % 2).wait()
     for side, x in ends:
+        inside = 1 if side == 0 else rows - 2
         for k, z in groups:
+            coeffs = tuple(coef[i, x, z] for i in range(5))
             for j in range(chunk):
                 u = tan[j, 0, x, z]
+                dv[j, x, z] = (
+                    gate_1[0, x, z] * u
+                    + plane(u, None, tan[j, 0, inside, z], coeffs)
+                    + DEPTH * depth_sum(lambda i: tan[j, 0, x, groups[i][1]], k, len(groups))
+                    + gate_1[1, x, z] * tan[j, 1, x, z]
+                    + jnp.where(reg[x, z] == step * chunk + j, gate_1[2, x, z], 0.0)
+                    - 0.1 * tan[j, 2, x, z]
+                )
                 state[side, 0, j, z] = 0.75 * tan[j, 1, x, z] + gate_1[3, x, z] * u
                 state[side, 1, j, z] = 0.096 * tan[j, 2, x, z] + 0.005 * u
+    for j in range(chunk):
+        now[j] = tan[j, 0, chip_outer]
+        later[j] = dv[j, chip_outer]
 
     def step_1(x):
         for k, z in groups:
@@ -233,6 +251,10 @@
                 dc[j, x, z] = 0.096 * tan[j, 2, x, z] + 0.005 * u
 
     pl.loop(1, rows - 1)(step_1)
+
+    @pl.when(step + 2 < count)
+    def _():
+        load(step + 2, step % 2).start()
 
     def step_2(x):
         for k, z in groups:
@@ -301,6 +323,10 @@
         far = signed(stencil_coeffs((sent - 1.0).astype(jnp.int32)), -sign)
         for i, at in enumerate((0, 3, 4)):
             coef[4 + i, z] = jnp.where(sent > 0.5, far[at], 0.0)
+
+    def stores(part):
+        pairs = ((dv.at[2], 0, outer), (dv.at[1], 0, inner), (dh, 1, outer), (dc, 2, outer))
+        return [pltpu.make_async_copy(a.at[part], out.at[part, f, x], sems.at[i]) for i, (a, f, x) in enumerate(pairs)]
 
     @pl.loop(0, fields // CHUNK)
     def _(step):
@@ -330,19 +356,9 @@
                 dh[p, z] = 0.75 * state[side, 0, p, z] + coef[3, z] * u
                 dc[p, z] = 9.6 * state[side, 1, p, z] + 0.05 * u
 
-    copies = [
-        pltpu.make_async_copy(ref, target, sems.at[i])
-        for i, (ref, target) in enumerate(
-            (
-                (dv.at[2], out.at[:, 0, outer]),
-                (dv.at[1], out.at[:, 0, inner]),
-                (dh, out.at[:, 1, outer]),
-                (dc, out.at[:, 2, outer]),
-            )
-        )
-    ]
-    for copy in copies:
-        copy.start()
+        for copy in stores(pl.ds(step * CHUNK, CHUNK)):
+            copy.start()
+
     count = laid.shape[0]
     first = side * (rows - count)
     lay_columns(lambda lanes: dv[2, :, :, lanes], laid, outer - first)
@@ -353,7 +369,7 @@
     take_columns(
         sites, laid, lines, first, lambda line: jnp.zeros_like(lines[line, :]) if before is None else before[line, :]
     )
-    for copy in copies:
+    for copy in stores(pl.ds(0, fields)):
         copy.wait()
 
 
@@ -384,14 +400,16 @@
         message_kernel,
         out_shape=message,
         in_specs=[smem, smem] + [hbm] * 5,
-        out_specs=vmem,
+        out_specs=hbm,
         scratch_shapes=[
+            pltpu.VMEM(message.shape, f32),
             pltpu.VMEM((fields,) + row, f32),
             pltpu.VMEM((2, fields) + row, f32),
             pltpu.VMEM(row, f32),
             pltpu.VMEM((2,) + row, jnp.int32),
             pltpu.VMEM((8,) + row, f32),
             pltpu.SemaphoreType.DMA((12,)),
+            pltpu.SemaphoreType.DMA((4,)),
         ],
         compiler_params=compiler_params(MESSAGE_MIB),
         cost_estimate=pl.CostEstimate(flops=1_000_000_000, bytes_accessed=MIB, transcendentals=0),
@@ -409,7 +427,6 @@
 
     field = pl.BlockSpec((rows,) + row, lambda i: (0, 0, 0))
     tan_spec = pl.BlockSpec((CHUNK, 3, rows) + row, lambda i: (i, 0, 0, 0, 0))
-    edge_spec = pl.BlockSpec((CHUNK,) + row, lambda i: (fields // CHUNK + i, 0, 0))
     tile = (rows,) + row
     partial_out, state, base_state, held, now, later, rest = pl.pallas_call(
         main_kernel,
@@ -423,7 +440,7 @@
             jax.ShapeDtypeStruct((fields,) + row, f32),
             jax.ShapeDtypeStruct((2,) + row, f32),
         ),
-        in_specs=[smem, smem] + [field] * 5 + [tan_spec, edge_spec],
+        in_specs=[smem, smem] + [field] * 5 + [hbm],
         out_specs=(
             tan_spec,
             pl.BlockSpec((2, 3, CHUNK) + row, lambda i: (0, 0, i, 0, 0)),
@@ -440,11 +457,13 @@
             pltpu.VMEM((CHUNK,) + tile, f32),
             pltpu.VMEM((CHUNK,) + tile, f32),
             pltpu.VMEM((CHUNK,) + tile, f32),
+            pltpu.VMEM((2, CHUNK, 3, rows) + row, f32),
+            pltpu.SemaphoreType.DMA((2,)),
         ],
-        compiler_params=compiler_params(36),
+        compiler_params=compiler_params(INTERIOR_MIB),
         cost_estimate=pl.CostEstimate(flops=1000, bytes_accessed=1024, transcendentals=0),
         name="interior",
-    )(chip_side, parameters, voltage, gating, recovery, region, fiber_class, tangents, over_link)
+    )(chip_side, parameters, voltage, gating, recovery, region, fiber_class, tangents)
     from_chip = tuple(swapped(part, 0, tiles) for part in (now, later, rest))
 
     def tail(side_at, filled, *messages):

time: 55.1 us -> 54.4 us (0.987)
  blocking collectives: 12.9 us -> 16 us
  Pallas kernels: 30.7 us -> 28.1 us
  local copies, waits for them, and re-layouts: 2.99 us -> 1.72 us
    all_to_all x1, blocking collectives: 12.9 us -> 16 us  [shards(): lax.all_to_all(outgoing.reshape(tiles, CAP, depth), 'tx', split_axis=0, c...]
    pallas_call x1, Pallas kernels: 16.1 us -> 14.5 us  [shards(): pl.pallas_call(main_kernel, grid=(fields // CHUNK,), out_shape=(jax.Shape...]
    unnamed x19, local copies, waits for them, and re-layouts: 2.99 us -> 1.72 us
    pallas_call x2, Pallas kernels: 10.6 us -> 10.1 us  [tail(): pl.pallas_call(tail_kernel, out_shape=(jax.ShapeDtypeStruct(tangents.shap...]
  transfers between devices with their start and end apart: 4 -> 4, of which waited for: 1 -> 1; matrix products, arithmetic and copies ran while one was open for 0% -> 0% of each run, Pallas kernels for 40% -> 36%
where the time goes in v4:
time: 54.4 us; the launch traced here: 54.2 us
  Pallas kernels  28.1 us (52%)
  blocking collectives  16 us (29%)
  starting transfers between devices  5.57 us (10%)
  local copies, waits for them, and re-layouts  1.72 us (3%)
  waiting for transfers between devices  1.69 us (3%)
  between operations  0.8 us (1%)
    all_to_all x1, blocking collectives, shards(): lax.all_to_all(outgoing.reshape(tiles, CAP, depth), 'tx', split_axis=0, c...  16 us
    pallas_call x1, Pallas kernels, shards(): pl.pallas_call(main_kernel, grid=(fields // CHUNK,), out_shape=(jax.Shape...  14.5 us
    pallas_call x2, Pallas kernels, tail(): pl.pallas_call(tail_kernel, out_shape=(jax.ShapeDtypeStruct(tangents.shap...  10.1 us
    ppermute x4, starting transfers between devices, swapped(): return lax.ppermute(message, 'tx', pairs + [(b, a) for a, b in pairs])  5.57 us
    pallas_call x1, Pallas kernels, shards(): pl.pallas_call(message_kernel, out_shape=message, in_specs=[smem, smem] +...  3.56 us
    unnamed x19, local copies, waits for them, and re-layouts  1.72 us
    ppermute x4, waiting for transfers between devices, swapped(): return lax.ppermute(message, 'tx', pairs + [(b, a) for a, b in pairs])  1.69 us
  transfers between devices with their start and end apart: 4, of which 1 were waited for; matrix products, arithmetic and copies ran while one was open for 0% of the time, Pallas kernels for 36%

profile of v4, /device:TPU:0, one launch (start us, length us, event | category | flops | bytes accessed | tf_op | source)
XLA Modules:
  0.0 54.2 jit_solution(4212675819934840024)
XLA Ops:
  0.6 0.0 copy-start.1
  0.7 0.0 copy-start.2
  0.7 0.0 copy-start.3
  0.7 0.0 copy-start.4
  0.7 0.0 copy-start.6
  0.7 3.6 %message.1.refs_0_ = f32[18,16,1024]{2,1,0:T(8,128)} custom-call(s32[1]{0:T(128)} %bitcast.side_at, f32[8]{0:T(128)} %params.3, f32[8,3,8,16,1024]{4,3,2,1,0:T(8,128)} %tan.1, f32[8,16,1024]{2,1,0:T(8,128)} %v.3, f32[8,16,1024]{2,1,0:T(8,128)} %h.3, s32[8,16,1024]{2,1,0:T(8,128)} %reg.3, s32[8,16,1024]{2,1,0:T(8,128)} %fib.3), custom_call_target="tpu_custom_call" | custom-call | flops 1000000000 | bytes 1048576 | tf_op jit(solution)/shard_map/message/pallas_call | solution.py:399
  4.3 0.7 %collective-permute-start.3 = (f32[18,16,1024]{2,1,0:T(8,128)}, f32[18,16,1024]{2,1,0:T(8,128)S(1)}, u32[]{:S(2)}, u32[]{:S(2)}) collective-permute-start(f32[18,16,1024]{2,1,0:T(8,128)} %message.1.refs_0_), channel_id=1, source_target_pairs={{1,2},{3,4},{5,6},{7,8},{9,10},{11,12},{13,14},{2,1},{4,3},{6,5},{... | collective-permute-start | bytes 3538952 | tf_op jit(solution)/shard_map/ppermute | solution.py:382
  5.0 0.0 copy-done.1
  5.0 0.0 copy-done.2
  5.0 0.0 copy-done.3
  5.0 0.0 copy-done.4
  5.0 0.0 copy-done.6
  5.1 0.0 copy-start.5
  5.1 1.0 %copy-done.5 = f32[8,16,1024]{2,1,0:T(8,128)S(1)} copy-done((f32[8,16,1024]{2,1,0:T(8,128)S(1)}, f32[8,16,1024]{2,1,0:T(8,128)}, u32[]{:S(2)}) %copy-start.5) | copy-done | bytes 524312
  6.1 0.0 copy-start.7
  6.1 14.5 %interior.1 = (f32[8,3,8,16,1024]{4,3,2,1,0:T(8,128)}, f32[2,3,8,16,1024]{4,3,2,1,0:T(8,128)S(1)}, f32[2,12,16,1024]{3,2,1,0:T(8,128)S(1)}, f32[8,6,16,1024]{3,2...) custom-call(s32[1]{0:T(128)} %bitcast.4.side_at, ...), custom_call_target="tpu_custom_call" | custom-call | flops 1000 | bytes 1024 | tf_op jit(solution)/shard_map/interior/pallas_call | solution.py:431
  20.6 4.3 %collective-permute-start = (f32[8,16,1024]{2,1,0:T(8,128)S(1)}, f32[8,16,1024]{2,1,0:T(8,128)S(1)}, u32[]{:S(2)}, u32[]{:S(2)}) collective-permute-start(f32[8,16,1024]{2,1,0:T(8,128)S(1)} %get-tuple-element.19.refs_0_), channel_id=1, source_target_pairs={{0,1},{2,3},{4,5},{6,7},{8,9},{10,11},{12,13},{14,15},{1,0},{3,2},... | collective-permute-start | bytes 1572872 | tf_op jit(solution)/shard_map/ppermute | solution.py:382
  24.9 0.1 collective-permute-start.1
  25.0 0.4 collective-permute-start.2
  25.4 0.0 copy-done.7
  25.4 0.1 convert_reduce_fusion
  25.6 0.0 copy-done.8
  25.6 0.1 select_reduce_fusion.sites
  25.7 1.7 %collective-permute-done.2.refs_4_ = f32[2,16,1024]{2,1,0:T(8,128)S(1)} collective-permute-done((f32[2,16,1024]{2,1,0:T(8,128)S(1)}, f32[2,16,1024]{2,1,0:T(8,128)S(1)}, u32[]{:S(2)}, u32[]{:S(2)}) %collective-permute-start.2) | collective-permute-done | bytes 131104 | tf_op jit(solution)/shard_map/ppermute | solution.py:382
  27.4 0.0 collective-permute-done.refs_2_
  27.4 0.0 collective-permute-done.1.refs_3_
  27.4 5.3 %tail.2 = (f32[8,3,8,16,1024]{4,3,2,1,0:T(8,128)}, f32[256,128]{1,0:T(8,128)S(1)}) custom-call(s32[1]{0:T(128)} %bitcast.4.side_at, s32[256]{0:T(256)S(1)} %select_reduce_fusion.sites, f32[2,3,8,16,1024]{4,3,2,1,0:T(8,128)S(1)} %get-tuple-element.15.state, f32[2,12,16,1024]{3,2,1,0:T(8,128)S(1)} %get-tuple-element.16.base_state, ...), custom_call_target="tpu_custom_call", output_to_operand_aliasing={{0}: (5, {})} | custom-call | flops 1000 | bytes 1024 | tf_op jit(solution)/shard_map/tail/pallas_call | solution.py:470
  32.7 0.0 collective-permute-done.3.refs_1_
  32.7 0.0 copy-done
  32.7 4.8 %tail.3 = (f32[8,3,8,16,1024]{4,3,2,1,0:T(8,128)}, f32[256,128]{1,0:T(8,128)S(1)}) custom-call(s32[1]{0:T(128)} %bitcast.side_at, s32[256]{0:T(256)S(1)} %select_reduce_fusion.sites, f32[2,3,8,16,1024]{4,3,2,1,0:T(8,128)S(1)} %get-tuple-element.15.state, f32[2,12,16,1024]{3,2,1,0:T(8,128)S(1)} %get-tuple-element.16.base_state, ...), custom_call_target="tpu_custom_call", output_to_operand_aliasing={{0}: (5, {})} | custom-call | flops 1000 | bytes 1024 | tf_op jit(solution)/shard_map/tail/pallas_call | solution.py:470
  37.5 16.0 %all_to_all.5 = f32[16,16,128]{2,1,0:T(8,128)S(1)} all-to-all(f32[16,16,128]{2,1,0:T(8,128)S(1)} %bitcast.7), channel_id=1, replica_groups=mesh['groups'=2,'tx'=16] {'tx'}, dimensions={0} | all-to-all | bytes 262144 | tf_op jit(solution)/shard_map/all_to_all | solution.py:493
  53.5 0.7 %copy.16 = f32[256,128]{1,0:T(8,128)} copy(f32[256,128]{1,0:T(8,128)S(1)} %bitcast.8) | data formatting | bytes 262144
  (3 shorter events, 0.0 us)
Async XLA Ops:
  0.6 4.4 %copy-start.1 = (f32[8,16,1024]{2,1,0:T(8,128)S(1)}, f32[8,16,1024]{2,1,0:T(8,128)}, u32[]{:S(2)}) copy-start(f32[8,16,1024]{2,1,0:T(8,128)} %v.3) | copy-start | bytes 1572868
  0.7 4.4 %copy-start.2 = (f32[8,16,1024]{2,1,0:T(8,128)S(1)}, f32[8,16,1024]{2,1,0:T(8,128)}, u32[]{:S(2)}) copy-start(f32[8,16,1024]{2,1,0:T(8,128)} %h.3) | copy-start | bytes 1572868
  0.7 4.4 %copy-start.3 = (s32[8,16,1024]{2,1,0:T(8,128)S(1)}, s32[8,16,1024]{2,1,0:T(8,128)}, u32[]{:S(2)}) copy-start(s32[8,16,1024]{2,1,0:T(8,128)} %reg.3) | copy-start | bytes 1572868
  0.7 4.4 %copy-start.4 = (s32[8,16,1024]{2,1,0:T(8,128)S(1)}, s32[8,16,1024]{2,1,0:T(8,128)}, u32[]{:S(2)}) copy-start(s32[8,16,1024]{2,1,0:T(8,128)} %fib.3) | copy-start | bytes 1572868
  0.7 4.4 %copy-start.6 = (f32[8]{0:T(128)S(1)}, f32[8]{0:T(128)}, u32[]{:S(2)}) copy-start(f32[8]{0:T(128)} %params.3) | copy-start | bytes 100
  4.3 28.4 %collective-permute-start.3 = (f32[18,16,1024]{2,1,0:T(8,128)}, f32[18,16,1024]{2,1,0:T(8,128)S(1)}, u32[]{:S(2)}, u32[]{:S(2)}) collective-permute-start(f32[18,16,1024]{2,1,0:T(8,128)} %message.1.refs_0_), channel_id=1, source_target_pairs={{1,2},{3,4},{5,6},{7,8},{9,10},{11,12},{13,14},{2,1},{4,3},{6,5},{... | collective-permute-start | bytes 3538952 | tf_op jit(solution)/shard_map/ppermute | solution.py:382
  5.1 1.0 %copy-start.5 = (f32[8,16,1024]{2,1,0:T(8,128)S(1)}, f32[8,16,1024]{2,1,0:T(8,128)}, u32[]{:S(2)}) copy-start(f32[8,16,1024]{2,1,0:T(8,128)} %c.1) | copy-start | bytes 1572868
  6.1 19.3 %copy-start.7 = (s32[256,1]{0,1:T(1,128)S(1)}, s32[256,1]{0,1:T(1,128)}, u32[]{:S(2)}) copy-start(s32[256,1]{0,1:T(1,128)} %param.17) | copy-start | bytes 3076
  6.1 19.5 %copy-start.8 = (s32[256]{0:T(256)S(1)}, s32[256]{0:T(256)}, u32[]{:S(2)}) copy-start(s32[256]{0:T(256)} %param.16) | copy-start | bytes 3076
  20.6 6.8 %collective-permute-start = (f32[8,16,1024]{2,1,0:T(8,128)S(1)}, f32[8,16,1024]{2,1,0:T(8,128)S(1)}, u32[]{:S(2)}, u32[]{:S(2)}) collective-permute-start(f32[8,16,1024]{2,1,0:T(8,128)S(1)} %get-tuple-element.19.refs_0_), channel_id=1, source_target_pairs={{0,1},{2,3},{4,5},{6,7},{8,9},{10,11},{12,13},{14,15},{1,0},{3,2},... | collective-permute-start | bytes 1572872 | tf_op jit(solution)/shard_map/ppermute | solution.py:382
  24.9 2.5 %collective-permute-start.1 = (f32[8,16,1024]{2,1,0:T(8,128)S(1)}, f32[8,16,1024]{2,1,0:T(8,128)S(1)}, u32[]{:S(2)}, u32[]{:S(2)}) collective-permute-start(f32[8,16,1024]{2,1,0:T(8,128)S(1)} %get-tuple-element.20.refs_1_), channel_id=1, source_target_pairs={{0,1},{2,3},{4,5},{6,7},{8,9},{10,11},{12,13},{14,15},{1,0},{3,2},... | collective-permute-start | bytes 1572872 | tf_op jit(solution)/shard_map/ppermute | solution.py:382
  25.0 2.4 %collective-permute-start.2 = (f32[2,16,1024]{2,1,0:T(8,128)S(1)}, f32[2,16,1024]{2,1,0:T(8,128)S(1)}, u32[]{:S(2)}, u32[]{:S(2)}) collective-permute-start(f32[2,16,1024]{2,1,0:T(8,128)S(1)} %get-tuple-element.21), channel_id=1, source_target_pairs={{0,1},{2,3},{4,5},{6,7},{8,9},{10,11},{12,13},{14,15},{1,0},{3,2},... | collective-permute-start | bytes 393224 | tf_op jit(solution)/shard_map/ppermute | solution.py:382
  27.4 5.3 %copy-start = (f32[18,16,1024]{2,1,0:T(8,128)S(1)}, f32[18,16,1024]{2,1,0:T(8,128)}, u32[]{:S(2)}) copy-start(f32[18,16,1024]{2,1,0:T(8,128)} %message.1.refs_0_) | copy-start | bytes 3538948

commit v5 on v4

--- a/solution.py
+++ b/solution.py
@@ -11,6 +11,7 @@
 GROUP = 8
 LANES = 128
 CHUNK = 2
+WIDE = 1
 MESSAGE_MIB = 54
 INTERIOR_MIB = 36
 MIB = 1 << 20
@@ -328,21 +329,21 @@
         pairs = ((dv.at[2], 0, outer), (dv.at[1], 0, inner), (dh, 1, outer), (dc, 2, outer))
         return [pltpu.make_async_copy(a.at[part], out.at[part, f, x], sems.at[i]) for i, (a, f, x) in enumerate(pairs)]
 
-    @pl.loop(0, fields // CHUNK)
+    @pl.loop(0, fields // WIDE)
     def _(step):
         for k, z in groups:
             own_row = tuple(base_state[side, i, z] for i in (0, 3, 4))
             next_row = tuple(base_state[side, 9 + i, z] for i in range(3))
-            for j in range(CHUNK):
-                p = step * CHUNK + j
+            for j in range(WIDE):
+                p = step * WIDE + j
                 extra = one_sided(far_now[p, z], *own_row)
                 dv[0, p, z] = later[p, z] + extra
                 dv[1, p, z] = held[p, inner - 1, z] + one_sided(extra, *next_row)
         for k, z in groups:
             coeffs = tuple(base_state[side, i, z] for i in range(5))
             far = tuple(coef[i, z] for i in (4, 5, 6))
-            for j in range(CHUNK):
-                p = step * CHUNK + j
+            for j in range(WIDE):
+                p = step * WIDE + j
                 u = dv[0, p, z]
                 outside = far_later[p, z] + one_sided(now[p, z], *far)
                 dv[2, p, z] = (
@@ -356,7 +357,7 @@
                 dh[p, z] = 0.75 * state[side, 0, p, z] + coef[3, z] * u
                 dc[p, z] = 9.6 * state[side, 1, p, z] + 0.05 * u
 
-        for copy in stores(pl.ds(step * CHUNK, CHUNK)):
+        for copy in stores(pl.ds(step * WIDE, WIDE)):
             copy.start()
 
     count = laid.shape[0]

time: 54.4 us -> 54.1 us (level)
  Pallas kernels: 28.1 us -> 27.4 us
    pallas_call x2, Pallas kernels: 10.1 us -> 9.4 us  [tail(): pl.pallas_call(tail_kernel, out_shape=(jax.ShapeDtypeStruct(tangents.shap...]
where the time goes in v5:
time: 54.1 us; the launch traced here: 53.9 us
  Pallas kernels  27.4 us (51%)
  blocking collectives  16.4 us (30%)
  starting transfers between devices  5.57 us (10%)
  local copies, waits for them, and re-layouts  1.72 us (3%)
  waiting for transfers between devices  1.69 us (3%)
  between operations  0.8 us (1%)
    all_to_all x1, blocking collectives, shards(): lax.all_to_all(outgoing.reshape(tiles, CAP, depth), 'tx', split_axis=0, c...  16.4 us
    pallas_call x1, Pallas kernels, shards(): pl.pallas_call(main_kernel, grid=(fields // CHUNK,), out_shape=(jax.Shape...  14.5 us
    pallas_call x2, Pallas kernels, tail(): pl.pallas_call(tail_kernel, out_shape=(jax.ShapeDtypeStruct(tangents.shap...  9.4 us
    ppermute x4, starting transfers between devices, swapped(): return lax.ppermute(message, 'tx', pairs + [(b, a) for a, b in pairs])  5.57 us
    pallas_call x1, Pallas kernels, shards(): pl.pallas_call(message_kernel, out_shape=message, in_specs=[smem, smem] +...  3.56 us
    unnamed x19, local copies, waits for them, and re-layouts  1.72 us
    ppermute x4, waiting for transfers between devices, swapped(): return lax.ppermute(message, 'tx', pairs + [(b, a) for a, b in pairs])  1.69 us
  transfers between devices with their start and end apart: 4, of which 1 were waited for; matrix products, arithmetic and copies ran while one was open for 0% of the time, Pallas kernels for 36%

profile of v5, /device:TPU:0, one launch (start us, length us, event | category | flops | bytes accessed | tf_op | source)
XLA Modules:
  0.0 53.9 jit_solution(12090892584062280548)
XLA Ops:
  0.6 0.0 copy-start.1
  0.7 0.0 copy-start.2
  0.7 0.0 copy-start.3
  0.7 0.0 copy-start.4
  0.7 0.0 copy-start.6
  0.7 3.6 %message.1.refs_0_ = f32[18,16,1024]{2,1,0:T(8,128)} custom-call(s32[1]{0:T(128)} %bitcast.side_at, f32[8]{0:T(128)} %params.3, f32[8,3,8,16,1024]{4,3,2,1,0:T(8,128)} %tan.1, f32[8,16,1024]{2,1,0:T(8,128)} %v.3, f32[8,16,1024]{2,1,0:T(8,128)} %h.3, s32[8,16,1024]{2,1,0:T(8,128)} %reg.3, s32[8,16,1024]{2,1,0:T(8,128)} %fib.3), custom_call_target="tpu_custom_call" | custom-call | flops 1000000000 | bytes 1048576 | tf_op jit(solution)/shard_map/message/pallas_call | solution.py:400
  4.3 0.7 %collective-permute-start.3 = (f32[18,16,1024]{2,1,0:T(8,128)}, f32[18,16,1024]{2,1,0:T(8,128)S(1)}, u32[]{:S(2)}, u32[]{:S(2)}) collective-permute-start(f32[18,16,1024]{2,1,0:T(8,128)} %message.1.refs_0_), channel_id=1, source_target_pairs={{1,2},{3,4},{5,6},{7,8},{9,10},{11,12},{13,14},{2,1},{4,3},{6,5},{... | collective-permute-start | bytes 3538952 | tf_op jit(solution)/shard_map/ppermute | solution.py:383
  5.0 0.0 copy-done.1
  5.0 0.0 copy-done.2
  5.0 0.0 copy-done.3
  5.0 0.0 copy-done.4
  5.0 0.0 copy-done.6
  5.1 0.0 copy-start.5
  5.1 1.0 %copy-done.5 = f32[8,16,1024]{2,1,0:T(8,128)S(1)} copy-done((f32[8,16,1024]{2,1,0:T(8,128)S(1)}, f32[8,16,1024]{2,1,0:T(8,128)}, u32[]{:S(2)}) %copy-start.5) | copy-done | bytes 524312
  6.1 0.0 copy-start.7
  6.1 14.5 %interior.1 = (f32[8,3,8,16,1024]{4,3,2,1,0:T(8,128)}, f32[2,3,8,16,1024]{4,3,2,1,0:T(8,128)S(1)}, f32[2,12,16,1024]{3,2,1,0:T(8,128)S(1)}, f32[8,6,16,1024]{3,2...) custom-call(s32[1]{0:T(128)} %bitcast.4.side_at, ...), custom_call_target="tpu_custom_call" | custom-call | flops 1000 | bytes 1024 | tf_op jit(solution)/shard_map/interior/pallas_call | solution.py:432
  20.6 4.3 %collective-permute-start = (f32[8,16,1024]{2,1,0:T(8,128)S(1)}, f32[8,16,1024]{2,1,0:T(8,128)S(1)}, u32[]{:S(2)}, u32[]{:S(2)}) collective-permute-start(f32[8,16,1024]{2,1,0:T(8,128)S(1)} %get-tuple-element.19.refs_0_), channel_id=1, source_target_pairs={{0,1},{2,3},{4,5},{6,7},{8,9},{10,11},{12,13},{14,15},{1,0},{3,2},... | collective-permute-start | bytes 1572872 | tf_op jit(solution)/shard_map/ppermute | solution.py:383
  24.9 0.1 collective-permute-start.1
  25.0 0.4 collective-permute-start.2
  25.4 0.0 copy-done.7
  25.4 0.1 convert_reduce_fusion
  25.6 0.0 copy-done.8
  25.6 0.1 select_reduce_fusion.sites
  25.7 1.7 %collective-permute-done.2.refs_4_ = f32[2,16,1024]{2,1,0:T(8,128)S(1)} collective-permute-done((f32[2,16,1024]{2,1,0:T(8,128)S(1)}, f32[2,16,1024]{2,1,0:T(8,128)S(1)}, u32[]{:S(2)}, u32[]{:S(2)}) %collective-permute-start.2) | collective-permute-done | bytes 131104 | tf_op jit(solution)/shard_map/ppermute | solution.py:383
  27.4 0.0 collective-permute-done.refs_2_
  27.4 0.0 collective-permute-done.1.refs_3_
  27.4 4.9 %tail.2 = (f32[8,3,8,16,1024]{4,3,2,1,0:T(8,128)}, f32[256,128]{1,0:T(8,128)S(1)}) custom-call(s32[1]{0:T(128)} %bitcast.4.side_at, s32[256]{0:T(256)S(1)} %select_reduce_fusion.sites, f32[2,3,8,16,1024]{4,3,2,1,0:T(8,128)S(1)} %get-tuple-element.15.state, f32[2,12,16,1024]{3,2,1,0:T(8,128)S(1)} %get-tuple-element.16.base_state, ...), custom_call_target="tpu_custom_call", output_to_operand_aliasing={{0}: (5, {})} | custom-call | flops 1000 | bytes 1024 | tf_op jit(solution)/shard_map/tail/pallas_call | solution.py:471
  32.3 0.0 collective-permute-done.3.refs_1_
  32.4 0.0 copy-done
  32.4 4.5 %tail.3 = (f32[8,3,8,16,1024]{4,3,2,1,0:T(8,128)}, f32[256,128]{1,0:T(8,128)S(1)}) custom-call(s32[1]{0:T(128)} %bitcast.side_at, s32[256]{0:T(256)S(1)} %select_reduce_fusion.sites, f32[2,3,8,16,1024]{4,3,2,1,0:T(8,128)S(1)} %get-tuple-element.15.state, f32[2,12,16,1024]{3,2,1,0:T(8,128)S(1)} %get-tuple-element.16.base_state, ...), custom_call_target="tpu_custom_call", output_to_operand_aliasing={{0}: (5, {})} | custom-call | flops 1000 | bytes 1024 | tf_op jit(solution)/shard_map/tail/pallas_call | solution.py:471
  36.8 16.4 %all_to_all.5 = f32[16,16,128]{2,1,0:T(8,128)S(1)} all-to-all(f32[16,16,128]{2,1,0:T(8,128)S(1)} %bitcast.7), channel_id=1, replica_groups=mesh['groups'=2,'tx'=16] {'tx'}, dimensions={0} | all-to-all | bytes 262144 | tf_op jit(solution)/shard_map/all_to_all | solution.py:494
  53.2 0.7 %copy.16 = f32[256,128]{1,0:T(8,128)} copy(f32[256,128]{1,0:T(8,128)S(1)} %bitcast.8) | data formatting | bytes 262144
  (3 shorter events, 0.0 us)
Async XLA Ops:
  0.6 4.4 %copy-start.1 = (f32[8,16,1024]{2,1,0:T(8,128)S(1)}, f32[8,16,1024]{2,1,0:T(8,128)}, u32[]{:S(2)}) copy-start(f32[8,16,1024]{2,1,0:T(8,128)} %v.3) | copy-start | bytes 1572868
  0.7 4.4 %copy-start.2 = (f32[8,16,1024]{2,1,0:T(8,128)S(1)}, f32[8,16,1024]{2,1,0:T(8,128)}, u32[]{:S(2)}) copy-start(f32[8,16,1024]{2,1,0:T(8,128)} %h.3) | copy-start | bytes 1572868
  0.7 4.4 %copy-start.3 = (s32[8,16,1024]{2,1,0:T(8,128)S(1)}, s32[8,16,1024]{2,1,0:T(8,128)}, u32[]{:S(2)}) copy-start(s32[8,16,1024]{2,1,0:T(8,128)} %reg.3) | copy-start | bytes 1572868
  0.7 4.4 %copy-start.4 = (s32[8,16,1024]{2,1,0:T(8,128)S(1)}, s32[8,16,1024]{2,1,0:T(8,128)}, u32[]{:S(2)}) copy-start(s32[8,16,1024]{2,1,0:T(8,128)} %fib.3) | copy-start | bytes 1572868
  0.7 4.4 %copy-start.6 = (f32[8]{0:T(128)S(1)}, f32[8]{0:T(128)}, u32[]{:S(2)}) copy-start(f32[8]{0:T(128)} %params.3) | copy-start | bytes 100
  4.3 28.1 %collective-permute-start.3 = (f32[18,16,1024]{2,1,0:T(8,128)}, f32[18,16,1024]{2,1,0:T(8,128)S(1)}, u32[]{:S(2)}, u32[]{:S(2)}) collective-permute-start(f32[18,16,1024]{2,1,0:T(8,128)} %message.1.refs_0_), channel_id=1, source_target_pairs={{1,2},{3,4},{5,6},{7,8},{9,10},{11,12},{13,14},{2,1},{4,3},{6,5},{... | collective-permute-start | bytes 3538952 | tf_op jit(solution)/shard_map/ppermute | solution.py:383
  5.1 1.0 %copy-start.5 = (f32[8,16,1024]{2,1,0:T(8,128)S(1)}, f32[8,16,1024]{2,1,0:T(8,128)}, u32[]{:S(2)}) copy-start(f32[8,16,1024]{2,1,0:T(8,128)} %c.1) | copy-start | bytes 1572868
  6.1 19.3 %copy-start.7 = (s32[256,1]{0,1:T(1,128)S(1)}, s32[256,1]{0,1:T(1,128)}, u32[]{:S(2)}) copy-start(s32[256,1]{0,1:T(1,128)} %param.17) | copy-start | bytes 3076
  6.1 19.5 %copy-start.8 = (s32[256]{0:T(256)S(1)}, s32[256]{0:T(256)}, u32[]{:S(2)}) copy-start(s32[256]{0:T(256)} %param.16) | copy-start | bytes 3076
  20.6 6.8 %collective-permute-start = (f32[8,16,1024]{2,1,0:T(8,128)S(1)}, f32[8,16,1024]{2,1,0:T(8,128)S(1)}, u32[]{:S(2)}, u32[]{:S(2)}) collective-permute-start(f32[8,16,1024]{2,1,0:T(8,128)S(1)} %get-tuple-element.19.refs_0_), channel_id=1, source_target_pairs={{0,1},{2,3},{4,5},{6,7},{8,9},{10,11},{12,13},{14,15},{1,0},{3,2},... | collective-permute-start | bytes 1572872 | tf_op jit(solution)/shard_map/ppermute | solution.py:383
  24.9 2.5 %collective-permute-start.1 = (f32[8,16,1024]{2,1,0:T(8,128)S(1)}, f32[8,16,1024]{2,1,0:T(8,128)S(1)}, u32[]{:S(2)}, u32[]{:S(2)}) collective-permute-start(f32[8,16,1024]{2,1,0:T(8,128)S(1)} %get-tuple-element.20.refs_1_), channel_id=1, source_target_pairs={{0,1},{2,3},{4,5},{6,7},{8,9},{10,11},{12,13},{14,15},{1,0},{3,2},... | collective-permute-start | bytes 1572872 | tf_op jit(solution)/shard_map/ppermute | solution.py:383
  25.0 2.4 %collective-permute-start.2 = (f32[2,16,1024]{2,1,0:T(8,128)S(1)}, f32[2,16,1024]{2,1,0:T(8,128)S(1)}, u32[]{:S(2)}, u32[]{:S(2)}) collective-permute-start(f32[2,16,1024]{2,1,0:T(8,128)S(1)} %get-tuple-element.21), channel_id=1, source_target_pairs={{0,1},{2,3},{4,5},{6,7},{8,9},{10,11},{12,13},{14,15},{1,0},{3,2},... | collective-permute-start | bytes 393224 | tf_op jit(solution)/shard_map/ppermute | solution.py:383
  27.4 5.0 %copy-start = (f32[18,16,1024]{2,1,0:T(8,128)S(1)}, f32[18,16,1024]{2,1,0:T(8,128)}, u32[]{:S(2)}) copy-start(f32[18,16,1024]{2,1,0:T(8,128)} %message.1.refs_0_) | copy-start | bytes 3538948

commit v6 on v5

--- a/solution.py
+++ b/solution.py
@@ -96,14 +96,14 @@
     fields, rows = tan.shape[0], tan.shape[2]
     groups = groups_of(tan.shape[3])
     outer, inner, sign = edge_of(side_at[0], rows)
-    half = fields // 2
+    half = fields // 4
     pairs = [
         (v.at[outer], out.at[2 * fields]),
         (h.at[outer], base),
         (reg.at[outer], label.at[0]),
         (fib.at[outer], label.at[1]),
     ]
-    for at in (0, half):
+    for at in range(0, fields, half):
         part = pl.ds(at, half)
         pairs += [
             (tan.at[part, 0, outer], out.at[part]),
@@ -130,7 +130,7 @@
         out[2 * fields + 1, z] = (fiber + 1).astype(jnp.float32)
     send(2 * fields, 2, 0).start()
 
-    for at in range(2):
+    for at in range(4):
         for copy in copies[4 + 4 * at : 8 + 4 * at]:
             copy.wait()
         send(at * half, half, 1 + at).start()
@@ -150,12 +150,12 @@
                         + jnp.where(label[0, z] == p, coef[7, z], 0.0)
                         - 0.1 * dhc[1, p, z]
                     )
-            send(fields + step * CHUNK, CHUNK, 3).start()
+            send(fields + step * CHUNK, CHUNK, 5).start()
 
     send(2 * fields, 2, 0).wait()
-    for at in range(2):
+    for at in range(4):
         send(at * half, half, 1 + at).wait()
-    send(fields, fields, 3).wait()
+    send(fields, fields, 5).wait()
 
 
 def main_kernel(
@@ -409,8 +409,8 @@
             pltpu.VMEM(row, f32),
             pltpu.VMEM((2,) + row, jnp.int32),
             pltpu.VMEM((8,) + row, f32),
-            pltpu.SemaphoreType.DMA((12,)),
-            pltpu.SemaphoreType.DMA((4,)),
+            pltpu.SemaphoreType.DMA((20,)),
+            pltpu.SemaphoreType.DMA((6,)),
         ],
         compiler_params=compiler_params(MESSAGE_MIB),
         cost_estimate=pl.CostEstimate(flops=1_000_000_000, bytes_accessed=MIB, transcendentals=0),

time: 54.1 us -> 54.1 us (level)
  no operation moved by 1% of the time
where the time goes in v6:
time: 54.1 us; the launch traced here: 53.9 us
  Pallas kernels  27.5 us (51%)
  blocking collectives  16.4 us (30%)
  starting transfers between devices  5.57 us (10%)
  local copies, waits for them, and re-layouts  1.72 us (3%)
  waiting for transfers between devices  1.69 us (3%)
  between operations  0.8 us (1%)
    all_to_all x1, blocking collectives, shards(): lax.all_to_all(outgoing.reshape(tiles, CAP, depth), 'tx', split_axis=0, c...  16.4 us
    pallas_call x1, Pallas kernels, shards(): pl.pallas_call(main_kernel, grid=(fields // CHUNK,), out_shape=(jax.Shape...  14.5 us
    pallas_call x2, Pallas kernels, tail(): pl.pallas_call(tail_kernel, out_shape=(jax.ShapeDtypeStruct(tangents.shap...  9.4 us
    ppermute x4, starting transfers between devices, swapped(): return lax.ppermute(message, 'tx', pairs + [(b, a) for a, b in pairs])  5.57 us
    pallas_call x1, Pallas kernels, shards(): pl.pallas_call(message_kernel, out_shape=message, in_specs=[smem, smem] +...  3.6 us
    unnamed x19, local copies, waits for them, and re-layouts  1.72 us
    ppermute x4, waiting for transfers between devices, swapped(): return lax.ppermute(message, 'tx', pairs + [(b, a) for a, b in pairs])  1.69 us
  transfers between devices with their start and end apart: 4, of which 1 were waited for; matrix products, arithmetic and copies ran while one was open for 0% of the time, Pallas kernels for 36%

profile of v6, /device:TPU:0, one launch (start us, length us, event | category | flops | bytes accessed | tf_op | source)
XLA Modules:
  0.0 53.9 jit_solution(5865928600779005346)
XLA Ops:
  0.6 0.0 copy-start.1
  0.7 0.0 copy-start.2
  0.7 0.0 copy-start.3
  0.7 0.0 copy-start.4
  0.7 0.0 copy-start.6
  0.7 3.6 %message.1.refs_0_ = f32[18,16,1024]{2,1,0:T(8,128)} custom-call(s32[1]{0:T(128)} %bitcast.side_at, f32[8]{0:T(128)} %params.3, f32[8,3,8,16,1024]{4,3,2,1,0:T(8,128)} %tan.1, f32[8,16,1024]{2,1,0:T(8,128)} %v.3, f32[8,16,1024]{2,1,0:T(8,128)} %h.3, s32[8,16,1024]{2,1,0:T(8,128)} %reg.3, s32[8,16,1024]{2,1,0:T(8,128)} %fib.3), custom_call_target="tpu_custom_call" | custom-call | flops 1000000000 | bytes 1048576 | tf_op jit(solution)/shard_map/message/pallas_call | solution.py:400
  4.3 0.7 %collective-permute-start.3 = (f32[18,16,1024]{2,1,0:T(8,128)}, f32[18,16,1024]{2,1,0:T(8,128)S(1)}, u32[]{:S(2)}, u32[]{:S(2)}) collective-permute-start(f32[18,16,1024]{2,1,0:T(8,128)} %message.1.refs_0_), channel_id=1, source_target_pairs={{1,2},{3,4},{5,6},{7,8},{9,10},{11,12},{13,14},{2,1},{4,3},{6,5},{... | collective-permute-start | bytes 3538952 | tf_op jit(solution)/shard_map/ppermute | solution.py:383
  5.0 0.0 copy-done.1
  5.0 0.0 copy-done.2
  5.1 0.0 copy-done.3
  5.1 0.0 copy-done.4
  5.1 0.0 copy-done.6
  5.1 0.0 copy-start.5
  5.1 1.0 %copy-done.5 = f32[8,16,1024]{2,1,0:T(8,128)S(1)} copy-done((f32[8,16,1024]{2,1,0:T(8,128)S(1)}, f32[8,16,1024]{2,1,0:T(8,128)}, u32[]{:S(2)}) %copy-start.5) | copy-done | bytes 524312
  6.1 0.0 copy-start.7
  6.1 14.5 %interior.1 = (f32[8,3,8,16,1024]{4,3,2,1,0:T(8,128)}, f32[2,3,8,16,1024]{4,3,2,1,0:T(8,128)S(1)}, f32[2,12,16,1024]{3,2,1,0:T(8,128)S(1)}, f32[8,6,16,1024]{3,2...) custom-call(s32[1]{0:T(128)} %bitcast.4.side_at, ...), custom_call_target="tpu_custom_call" | custom-call | flops 1000 | bytes 1024 | tf_op jit(solution)/shard_map/interior/pallas_call | solution.py:432
  20.6 4.3 %collective-permute-start = (f32[8,16,1024]{2,1,0:T(8,128)S(1)}, f32[8,16,1024]{2,1,0:T(8,128)S(1)}, u32[]{:S(2)}, u32[]{:S(2)}) collective-permute-start(f32[8,16,1024]{2,1,0:T(8,128)S(1)} %get-tuple-element.19.refs_0_), channel_id=1, source_target_pairs={{0,1},{2,3},{4,5},{6,7},{8,9},{10,11},{12,13},{14,15},{1,0},{3,2},... | collective-permute-start | bytes 1572872 | tf_op jit(solution)/shard_map/ppermute | solution.py:383
  25.0 0.1 collective-permute-start.1
  25.0 0.4 collective-permute-start.2
  25.5 0.0 copy-done.7
  25.5 0.1 convert_reduce_fusion
  25.6 0.0 copy-done.8
  25.6 0.1 select_reduce_fusion.sites
  25.8 1.7 %collective-permute-done.2.refs_4_ = f32[2,16,1024]{2,1,0:T(8,128)S(1)} collective-permute-done((f32[2,16,1024]{2,1,0:T(8,128)S(1)}, f32[2,16,1024]{2,1,0:T(8,128)S(1)}, u32[]{:S(2)}, u32[]{:S(2)}) %collective-permute-start.2) | collective-permute-done | bytes 131104 | tf_op jit(solution)/shard_map/ppermute | solution.py:383
  27.4 0.0 collective-permute-done.refs_2_
  27.4 0.0 collective-permute-done.1.refs_3_
  27.4 4.9 %tail.2 = (f32[8,3,8,16,1024]{4,3,2,1,0:T(8,128)}, f32[256,128]{1,0:T(8,128)S(1)}) custom-call(s32[1]{0:T(128)} %bitcast.4.side_at, s32[256]{0:T(256)S(1)} %select_reduce_fusion.sites, f32[2,3,8,16,1024]{4,3,2,1,0:T(8,128)S(1)} %get-tuple-element.15.state, f32[2,12,16,1024]{3,2,1,0:T(8,128)S(1)} %get-tuple-element.16.base_state, ...), custom_call_target="tpu_custom_call", output_to_operand_aliasing={{0}: (5, {})} | custom-call | flops 1000 | bytes 1024 | tf_op jit(solution)/shard_map/tail/pallas_call | solution.py:471
  32.4 0.0 collective-permute-done.3.refs_1_
  32.4 0.0 copy-done
  32.4 4.5 %tail.3 = (f32[8,3,8,16,1024]{4,3,2,1,0:T(8,128)}, f32[256,128]{1,0:T(8,128)S(1)}) custom-call(s32[1]{0:T(128)} %bitcast.side_at, s32[256]{0:T(256)S(1)} %select_reduce_fusion.sites, f32[2,3,8,16,1024]{4,3,2,1,0:T(8,128)S(1)} %get-tuple-element.15.state, f32[2,12,16,1024]{3,2,1,0:T(8,128)S(1)} %get-tuple-element.16.base_state, ...), custom_call_target="tpu_custom_call", output_to_operand_aliasing={{0}: (5, {})} | custom-call | flops 1000 | bytes 1024 | tf_op jit(solution)/shard_map/tail/pallas_call | solution.py:471
  36.9 16.4 %all_to_all.5 = f32[16,16,128]{2,1,0:T(8,128)S(1)} all-to-all(f32[16,16,128]{2,1,0:T(8,128)S(1)} %bitcast.7), channel_id=1, replica_groups=mesh['groups'=2,'tx'=16] {'tx'}, dimensions={0} | all-to-all | bytes 262144 | tf_op jit(solution)/shard_map/all_to_all | solution.py:494
  53.2 0.7 %copy.16 = f32[256,128]{1,0:T(8,128)} copy(f32[256,128]{1,0:T(8,128)S(1)} %bitcast.8) | data formatting | bytes 262144
  (3 shorter events, 0.0 us)
Async XLA Ops:
  0.6 4.4 %copy-start.1 = (f32[8,16,1024]{2,1,0:T(8,128)S(1)}, f32[8,16,1024]{2,1,0:T(8,128)}, u32[]{:S(2)}) copy-start(f32[8,16,1024]{2,1,0:T(8,128)} %v.3) | copy-start | bytes 1572868
  0.7 4.4 %copy-start.2 = (f32[8,16,1024]{2,1,0:T(8,128)S(1)}, f32[8,16,1024]{2,1,0:T(8,128)}, u32[]{:S(2)}) copy-start(f32[8,16,1024]{2,1,0:T(8,128)} %h.3) | copy-start | bytes 1572868
  0.7 4.4 %copy-start.3 = (s32[8,16,1024]{2,1,0:T(8,128)S(1)}, s32[8,16,1024]{2,1,0:T(8,128)}, u32[]{:S(2)}) copy-start(s32[8,16,1024]{2,1,0:T(8,128)} %reg.3) | copy-start | bytes 1572868
  0.7 4.4 %copy-start.4 = (s32[8,16,1024]{2,1,0:T(8,128)S(1)}, s32[8,16,1024]{2,1,0:T(8,128)}, u32[]{:S(2)}) copy-start(s32[8,16,1024]{2,1,0:T(8,128)} %fib.3) | copy-start | bytes 1572868
  0.7 4.4 %copy-start.6 = (f32[8]{0:T(128)S(1)}, f32[8]{0:T(128)}, u32[]{:S(2)}) copy-start(f32[8]{0:T(128)} %params.3) | copy-start | bytes 100
  4.3 28.1 %collective-permute-start.3 = (f32[18,16,1024]{2,1,0:T(8,128)}, f32[18,16,1024]{2,1,0:T(8,128)S(1)}, u32[]{:S(2)}, u32[]{:S(2)}) collective-permute-start(f32[18,16,1024]{2,1,0:T(8,128)} %message.1.refs_0_), channel_id=1, source_target_pairs={{1,2},{3,4},{5,6},{7,8},{9,10},{11,12},{13,14},{2,1},{4,3},{6,5},{... | collective-permute-start | bytes 3538952 | tf_op jit(solution)/shard_map/ppermute | solution.py:383
  5.1 1.0 %copy-start.5 = (f32[8,16,1024]{2,1,0:T(8,128)S(1)}, f32[8,16,1024]{2,1,0:T(8,128)}, u32[]{:S(2)}) copy-start(f32[8,16,1024]{2,1,0:T(8,128)} %c.1) | copy-start | bytes 1572868
  6.1 19.3 %copy-start.7 = (s32[256,1]{0,1:T(1,128)S(1)}, s32[256,1]{0,1:T(1,128)}, u32[]{:S(2)}) copy-start(s32[256,1]{0,1:T(1,128)} %param.17) | copy-start | bytes 3076
  6.1 19.5 %copy-start.8 = (s32[256]{0:T(256)S(1)}, s32[256]{0:T(256)}, u32[]{:S(2)}) copy-start(s32[256]{0:T(256)} %param.16) | copy-start | bytes 3076
  20.6 6.8 %collective-permute-start = (f32[8,16,1024]{2,1,0:T(8,128)S(1)}, f32[8,16,1024]{2,1,0:T(8,128)S(1)}, u32[]{:S(2)}, u32[]{:S(2)}) collective-permute-start(f32[8,16,1024]{2,1,0:T(8,128)S(1)} %get-tuple-element.19.refs_0_), channel_id=1, source_target_pairs={{0,1},{2,3},{4,5},{6,7},{8,9},{10,11},{12,13},{14,15},{1,0},{3,2},... | collective-permute-start | bytes 1572872 | tf_op jit(solution)/shard_map/ppermute | solution.py:383
  25.0 2.5 %collective-permute-start.1 = (f32[8,16,1024]{2,1,0:T(8,128)S(1)}, f32[8,16,1024]{2,1,0:T(8,128)S(1)}, u32[]{:S(2)}, u32[]{:S(2)}) collective-permute-start(f32[8,16,1024]{2,1,0:T(8,128)S(1)} %get-tuple-element.20.refs_1_), channel_id=1, source_target_pairs={{0,1},{2,3},{4,5},{6,7},{8,9},{10,11},{12,13},{14,15},{1,0},{3,2},... | collective-permute-start | bytes 1572872 | tf_op jit(solution)/shard_map/ppermute | solution.py:383
  25.0 2.4 %collective-permute-start.2 = (f32[2,16,1024]{2,1,0:T(8,128)S(1)}, f32[2,16,1024]{2,1,0:T(8,128)S(1)}, u32[]{:S(2)}, u32[]{:S(2)}) collective-permute-start(f32[2,16,1024]{2,1,0:T(8,128)S(1)} %get-tuple-element.21), channel_id=1, source_target_pairs={{0,1},{2,3},{4,5},{6,7},{8,9},{10,11},{12,13},{14,15},{1,0},{3,2},... | collective-permute-start | bytes 393224 | tf_op jit(solution)/shard_map/ppermute | solution.py:383
  27.4 5.0 %copy-start = (f32[18,16,1024]{2,1,0:T(8,128)S(1)}, f32[18,16,1024]{2,1,0:T(8,128)}, u32[]{:S(2)}) copy-start(f32[18,16,1024]{2,1,0:T(8,128)} %message.1.refs_0_) | copy-start | bytes 3538948
